TPU v7x, 256 devices: a whole 4x4x8 slice. The times are simulated.
256 devices in a mesh: ctx: 64 (over y, x_lo, z), tp: 4 (over x_hi, core).
Axes of the slice: x: 4 (x_hi: 2, x_lo: 2; x = x_hi * 2 + x_lo), y: 4, z: 8, core: 2. Of those that a mesh axis runs over, the one named last changes fastest.
Arguments:
- tokens: bfloat16 [32768, 4096], P(('ctx', 'tp')), may hold values from -20 to 20
- norm_gain: float32 [4096], replicated, may hold values from 0.1 to 1.9
- w_query: bfloat16 [4096, 4096], P('ctx', 'tp'), may hold values from -1 to 1
- w_key: bfloat16 [4096, 512], P('ctx', 'tp'), may hold values from -16 to 16
- w_value: bfloat16 [4096, 512], P('ctx', 'tp'), may hold values from -0.09375 to 0.09375
- w_out: bfloat16 [4096, 4096], P('tp', 'ctx'), may hold values from -0.375 to 0.375
- doc_blocks: int32 [256], replicated, may hold values from 0 to 35, never falling along the last dimension, each value on 1 to 12 neighbouring positions
Outputs:
- attention_out: bfloat16 [32768, 4096], P(('ctx', 'tp'))
Inputs may be any that keep to these rules, and one draw needn't show every extreme that they name: doc_blocks never falls; every document spans 1 to 12 blocks, and one spans exactly 12.
All inputs are finite; a program needn't handle non-finite values.
Results may differ from a plain program's by a relative error of at most 0.019.
Values may be sent and summed in bfloat16 or wider, within the bound.
A program may use at most 128 MiB of HBM per device.

v0:
```python
import jax
import jax.numpy as jnp
from jax import lax
from jax.sharding import PartitionSpec as P

HD = 128
BLOCK = 128
SPAN = 4


rope_base = 500000.0
neg_large = -1e30


def passed_along(value, axis, steps):
    count = lax.axis_size(axis)
    leading, last = (max(0, -steps), min(count, count - steps))
    return lax.ppermute(value, axis, [(source, source + steps) for source in range(leading, last)])


def rotate(values, positions):
    half_width = values.shape[-1] // 2
    frequency = rope_base ** (-jnp.arange(half_width, dtype=jnp.float32) / half_width)
    angles = positions.astype(jnp.float32)[:, None] * frequency[None, :]
    cosine = jnp.cos(angles)[:, None, :]
    sine_part = jnp.sin(angles)[:, None, :]
    first_half = values[..., :half_width]
    second_half = values[..., half_width:]
    return jnp.concatenate(
        [
            first_half * cosine - second_half * sine_part,
            second_half * cosine + first_half * sine_part,
        ],
        axis=-1,
    )


def doc_ranks(doc_blocks, source, per_device):
    start_block = jnp.maximum(source, 0) * per_device
    block_docs = lax.dynamic_slice_in_dim(doc_blocks, start_block, per_device, 0)
    block_docs = jnp.where(source >= 0, block_docs, -1)
    return jnp.repeat(block_docs, BLOCK, total_repeat_length=per_device * BLOCK)


def attend(attn_state, query_heads, key_block, value_block, query_docs, key_docs, causal):
    running_max, running_sum, running_out = attn_state
    scores = jnp.einsum(
        "qkgd,skd->qkgs", query_heads, key_block, preferred_element_type=jnp.float32
    )
    visible = query_docs[:, None] == key_docs[None, :]
    if causal is not None:
        visible = visible & causal
    visible = visible[:, None, None, :]
    scores = jnp.where(visible, scores, neg_large)
    new_max = jnp.maximum(running_max, jnp.max(scores, axis=-1))
    factor = jnp.exp(running_max - new_max)
    weights = jnp.where(visible, jnp.exp(scores - new_max[..., None]), 0.0).astype(jnp.bfloat16)
    new_sum = running_sum * factor + jnp.sum(weights, axis=-1, dtype=jnp.float32)
    new_out = running_out * factor[..., None] + jnp.einsum(
        "qkgs,skd->qkgd", weights, value_block, preferred_element_type=jnp.float32
    )
    return (new_max, new_sum, new_out)


def local(tokens, norm_gain, w_query, w_key, w_value, w_out, doc_blocks):
    ctx_index = lax.axis_index("ctx")
    token_float = tokens.astype(jnp.float32)
    scale_inv = lax.rsqrt(jnp.mean(token_float * token_float, axis=-1, keepdims=True) + 1e-05)
    normed = (token_float * scale_inv * norm_gain).astype(jnp.bfloat16)
    context_rows = lax.all_gather(normed, "tp", axis=0, tiled=True)
    row_count = context_rows.shape[0]
    query_sum = jnp.dot(
        context_rows,
        lax.all_gather(w_query, "ctx", axis=0, tiled=True),
        preferred_element_type=jnp.float32,
    )
    key_sum = jnp.dot(
        context_rows,
        lax.all_gather(w_key, "ctx", axis=0, tiled=True),
        preferred_element_type=jnp.float32,
    )
    value_sum = jnp.dot(
        context_rows,
        lax.all_gather(w_value, "ctx", axis=0, tiled=True),
        preferred_element_type=jnp.float32,
    )
    kv_local = w_key.shape[1] // HD
    group_size = w_query.shape[1] // w_key.shape[1]
    positions = ctx_index * row_count + jnp.arange(row_count, dtype=jnp.int32)
    query_heads = (
        rotate(query_sum.reshape(row_count, kv_local * group_size, HD), positions) * HD ** (-0.5)
    ).astype(jnp.bfloat16)
    query_heads = query_heads.reshape(row_count, kv_local, group_size, HD)
    key_heads = rotate(key_sum.reshape(row_count, kv_local, HD), positions).astype(jnp.bfloat16)
    value_heads = value_sum.reshape(row_count, kv_local, HD).astype(jnp.bfloat16)
    kv_local_pair = jnp.stack([key_heads, value_heads])
    per_device = row_count // BLOCK
    query_docs = doc_ranks(doc_blocks, ctx_index, per_device)
    row_iota = jnp.arange(row_count, dtype=jnp.int32)
    causal = row_iota[:, None] >= row_iota[None, :]
    init_state = (
        jnp.full((row_count, kv_local, group_size), neg_large, jnp.float32),
        jnp.zeros((row_count, kv_local, group_size), jnp.float32),
        jnp.zeros((row_count, kv_local, group_size, HD), jnp.float32),
    )
    attn_state = attend(
        init_state, query_heads, key_heads, value_heads, query_docs, query_docs, causal
    )

    def remote(current_state, distance, kv_block):
        key_docs = doc_ranks(doc_blocks, ctx_index - distance, per_device)
        return attend(
            current_state, query_heads, kv_block[0], kv_block[1], query_docs, key_docs, None
        )

    def relay_turn(turn_index, loop_carry):
        current_state, moving = loop_carry
        moving = passed_along(moving, "ctx", 1)
        return (remote(current_state, turn_index + 1, moving), moving)

    attn_state, moving = lax.fori_loop(0, SPAN - 1, relay_turn, (attn_state, kv_local_pair))
    final_max, final_sum, final_out = attn_state
    attended = (
        (final_out / final_sum[..., None])
        .reshape(row_count, kv_local * group_size * HD)
        .astype(jnp.bfloat16)
    )
    partial_out = jnp.dot(
        attended,
        lax.all_gather(w_out, "ctx", axis=1, tiled=True),
        preferred_element_type=jnp.float32,
    )
    summed = lax.psum_scatter(
        partial_out.astype(jnp.bfloat16), "tp", scatter_dimension=0, tiled=True
    )
    return summed


def solution(mesh):
    return jax.shard_map(
        local,
        mesh=mesh,
        in_specs=(
            P(("ctx", "tp"), None),
            P(),
            P("ctx", "tp"),
            P("ctx", "tp"),
            P("ctx", "tp"),
            P("tp", "ctx"),
            P(),
        ),
        out_specs=P(("ctx", "tp"), None),
        check_vma=False,
    )
```

profile of v0, /device:TPU:38, one launch (start us, length us, event | category | flops | bytes accessed | tf_op | source)
XLA Modules:
  0.0 1337.7 jit_solution(12687959731255810308)
XLA Ops:
  8.8 2.5 fusion.13
  14.1 2.5 select_select_fusion.1
  17.8 277.1 %all-gather.8.cloned.1.call-done = bf16[4096,128]{1,0:T(8,128)(2,1)} async-done(((bf16[64,128]{1,0:T(8,128)(2,1)}), bf16[4096,128]{1,0:T(8,128)(2,1)}) %all-gather.8.cloned.1.call-update) | async-done | bytes 1048592 | tf_op jit(solution)/shard_map/all_gather | solution.py:79
  294.9 52.2 %all-gather.6.cloned.1.call-done = bf16[512,4096]{1,0:T(8,128)(2,1)} async-done(((bf16[128,4096]{1,0:T(8,128)(2,1)}), bf16[512,4096]{1,0:T(8,128)(2,1)}) %all-gather.6.cloned.1.call-update) | async-done | bytes 4194320 | tf_op jit(solution)/shard_map/all_gather | solution.py:70
  347.2 4.0 convolution_bitcast_fusion.1
  351.7 281.5 %all-gather.12.cloned.1.call-done = bf16[4096,128]{1,0:T(8,128)(2,1)} async-done(((bf16[64,128]{1,0:T(8,128)(2,1)}), bf16[4096,128]{1,0:T(8,128)(2,1)}) %all-gather.12.cloned.1.call-update) | async-done | bytes 1048592 | tf_op jit(solution)/shard_map/all_gather | solution.py:84
  633.2 4.0 convolution_convert_fusion.1
  638.1 306.2 %all-gather.10.cloned.1.call-done = bf16[4096,1024]{1,0:T(8,128)(2,1)} async-done(((bf16[64,1024]{1,0:T(8,128)(2,1)}), bf16[4096,1024]{1,0:T(8,128)(2,1)}) %all-gather.10.cloned.1.call-update) | async-done | bytes 8388624 | tf_op jit(solution)/shard_map/all_gather | solution.py:74
  944.3 8.1 convolution_bitcast_fusion
  956.3 3.2 copy-done
  959.5 3.6 fusion.16
  963.1 2.9 copy.22
  968.3 5.3 convert_reduce_fusion.1
  973.6 55.0 %while.25 = (s32[]{:T(128)}, f32[512,1,8]{0,2,1:T(8,128)S(1)}, f32[512,1,8]{0,2,1:T(8,128)S(1)}, f32[512,1,8,128]{3,0,2,1:T(8,128)S(1)}, bf16[2,512,1,128]{3,1,2...) while((s32[]{:T(128)}, f32[512,1,8]{0,2,1:T(8,128)S(1)}, ...), condition=%wide.region_6.8_spmd, body=%wide.region_3.7_spmd.sunk | while | flops 1100238336 | bytes 33560904 | solution.py:121
  973.8 2.5 collective-permute-start
  979.6 5.2 collective-permute-done
  988.6 2.8 bitcast_add_fusion.7
  996.7 6.9 collective-permute-done
  1007.4 2.8 bitcast_add_fusion.7
  1015.4 6.5 collective-permute-done
  1025.7 2.8 bitcast_add_fusion.7
  1032.3 222.9 %all-gather.14.cloned.1.call-done = bf16[1024,4096]{0,1:T(8,128)(2,1)} async-done(((bf16[1024,64]{0,1:T(8,128)(2,1)}), bf16[1024,4096]{0,1:T(8,128)(2,1)}) %all-gather.14.cloned.1.call-update) | async-done | bytes 8388624 | tf_op jit(solution)/shard_map/all_gather | solution.py:130
  1255.2 9.6 convolution_convert_fusion
  1264.9 65.9 %reduce-scatter.2.cloned.1.call-done = bf16[128,4096]{1,0:T(8,128)(2,1)} async-done(((bf16[512,4096]{1,0:T(8,128)(2,1)}), bf16[128,4096]{1,0:T(8,128)(2,1)}) %reduce-scatter.2.cloned.1.call-update) | async-done | bytes 1048592 | tf_op jit(solution)/shard_map/reduce_scatter | solution.py:133
  (71 shorter events, 42.2 us)
Async XLA Ops:
  6.5 6.8 copy-start.3
  6.5 288.4 %all-gather.8.cloned.1.call-start = ((), (), s32[]{:S(2)}) async-start(), calls=%async_computation.2 | async-start | bytes 1064960 | tf_op jit(solution)/shard_map/all_gather | solution.py:79
  7.3 339.9 %all-gather.6.cloned.1.call-start = ((), (), s32[]{:S(2)}) async-start(), calls=%async_computation.1 | async-start | bytes 5242880 | tf_op jit(solution)/shard_map/all_gather | solution.py:70
  11.4 621.8 %all-gather.12.cloned.1.call-start = ((), (), s32[]{:S(2)}) async-start(), calls=%async_computation.4 | async-start | bytes 1064960 | tf_op jit(solution)/shard_map/all_gather | solution.py:84
  12.1 932.2 %all-gather.10.cloned.1.call-start = ((), (), s32[]{:S(2)}) async-start(), calls=%async_computation.3 | async-start | bytes 8519680 | tf_op jit(solution)/shard_map/all_gather | solution.py:74
  12.7 1242.5 %all-gather.14.cloned.1.call-start = ((), (), s32[]{:S(2)}) async-start(), calls=%async_computation.5 | async-start | bytes 8519680 | tf_op jit(solution)/shard_map/all_gather | solution.py:130
  13.3 1317.5 %reduce-scatter.2.cloned.1.call-start = ((), (), s32[]{:S(2)}) async-start(), calls=%async_computation.6 | async-start | bytes 5242880 | tf_op jit(solution)/shard_map/reduce_scatter | solution.py:133
  954.4 1.9 copy-start.1
  956.3 3.2 copy-start
  968.3 5.3 copy-start.2
  973.8 11.0 collective-permute-start
  991.5 12.1 collective-permute-start
  1010.2 11.7 collective-permute-start
Sparse Core Ops, SparseCore 0:
  9.1 285.7 all-gather.7
  296.8 50.3 all-gather.5
  349.0 284.2 all-gather.11
  634.9 309.4 all-gather.9
  946.0 309.1 all-gather.13
  1265.0 65.7 reduce-scatter.1
where the time goes:
time: 1340 us
  waiting for transfers between devices  1230 us (92%)
  matrix products  43.7 us (3%)
  other arithmetic  31.7 us (2%)
  local copies, waits for them, and re-layouts  14.5 us (1%)
  between operations  13.7 us (1%)
    all_gather x1, waiting for transfers between devices, local(): lax.all_gather(w_query, 'ctx', axis=0, tiled=True)  306 us
    all_gather x1, waiting for transfers between devices, local(): lax.all_gather(w_value, 'ctx', axis=0, tiled=True)  281 us
    all_gather x1, waiting for transfers between devices, local(): lax.all_gather(w_key, 'ctx', axis=0, tiled=True)  277 us
    all_gather x1, waiting for transfers between devices, local(): lax.all_gather(w_out, 'ctx', axis=1, tiled=True)  223 us
    reduce_scatter x1, waiting for transfers between devices, local(): lax.psum_scatter(partial_out.astype(jnp.bfloat16), 'tp', scatter_dimensio...  65.9 us
    all_gather x1, waiting for transfers between devices, local(): context_rows = lax.all_gather(normed, 'tp', axis=0, tiled=True)  52.2 us
  transfers between devices with their start and end apart: 9, of which 9 were waited for; matrix products, arithmetic and copies ran while one was open for 6% of the time, Pallas kernels for 0%

commit v1 on v0

--- a/solution.py
+++ b/solution.py
@@ -1,15 +1,207 @@
+import functools
+
 import jax
 import jax.numpy as jnp
 from jax import lax
+from jax.experimental import pallas as pl
+from jax.experimental.pallas import tpu as pltpu
 from jax.sharding import PartitionSpec as P
 
 HD = 128
 BLOCK = 128
 SPAN = 4
-
+NY, NX, NZ = 4, 2, 8
+MESH = pl.DeviceIdType.MESH
 
 rope_base = 500000.0
 neg_large = -1e30
+
+Z_OFFSETS = [0, -1, 1, -2, 2, -3, 3, 4]
+Y_OFFSETS = [0, -1, 1, 2]
+COPIES_A = 1 + 8 + 32
+COPIES_B = 1 + 4 + 32
+
+
+def place():
+    c = lax.axis_index("ctx")
+    return c // (NX * NZ), lax.rem(c // NZ, NX), lax.rem(c, NZ)
+
+
+def ctx_of(y, x, z):
+    return (lax.rem(y + NY, NY) * NX + x) * NZ + lax.rem(z + NZ, NZ)
+
+
+class Gather:
+    def __init__(self, buf, send_sems, recv_sems, first, z_first):
+        self.buf, self.send_sems, self.recv_sems = buf, send_sems, recv_sems
+        self.y, self.x, self.z = place()
+        self.first, self.z_first = first, z_first
+        self.sent = []
+
+    def copy(self, index, yy, zz, half, to):
+        yy, zz = lax.rem(yy + 2 * NY, NY), lax.rem(zz + 2 * NZ, NZ)
+        if half is None:
+            ref = self.buf.at[yy, :, zz]
+        else:
+            ref = self.buf.at[yy, half, zz]
+        return pltpu.make_async_remote_copy(
+            src_ref=ref,
+            dst_ref=ref,
+            send_sem=self.send_sems.at[self.first + index],
+            recv_sem=self.recv_sems.at[self.first + index],
+            device_id={"ctx": ctx_of(*to)},
+            device_id_type=MESH,
+        )
+
+    def ring_id(self, second, block, direction, hop, length):
+        half_way = length // 2
+        base = 1 if not second else 1 + 2 * (NZ if self.z_first else NY) // 2 + block * length
+        return base + (0 if direction > 0 else half_way) + hop - 1
+
+    def ring_copy(self, second, block, direction, hop):
+        raise NotImplementedError
+
+    def along_z(self, second, y_offset, block, direction, hop, sending):
+        distance = hop - 1 if sending else hop
+        half = (0 if direction > 0 else 1) if hop == NZ // 2 else None
+        return self.copy(
+            self.ring_id(second, block, direction, hop, NZ),
+            self.y + y_offset,
+            self.z - direction * distance,
+            half,
+            (self.y, self.x, self.z + direction),
+        )
+
+    def along_y(self, second, z_offset, block, direction, hop, sending):
+        distance = hop - 1 if sending else hop
+        half = (0 if direction > 0 else 1) if hop == NY // 2 else None
+        return self.copy(
+            self.ring_id(second, block, direction, hop, NY),
+            self.y - direction * distance,
+            self.z + z_offset,
+            half,
+            (self.y + direction, self.x, self.z),
+        )
+
+    def send(self, copy):
+        copy.start()
+        self.sent.append(copy)
+
+    def first_ring(self, direction, hop, sending):
+        if self.z_first:
+            return self.along_z(False, 0, 0, direction, hop, sending)
+        return self.along_y(False, 0, 0, direction, hop, sending)
+
+    def second_ring(self, block, direction, hop, sending):
+        if self.z_first:
+            return self.along_y(True, Z_OFFSETS[block], block, direction, hop, sending)
+        return self.along_z(True, Y_OFFSETS[block], block, direction, hop, sending)
+
+    def exchange(self):
+        copy = self.copy(0, self.y, self.z, self.x, (self.y, 1 - self.x, self.z))
+        self.send(copy)
+
+    def begin(self):
+        self.copy(0, self.y, self.z, 1 - self.x, (self.y, 1 - self.x, self.z)).wait_recv()
+        for direction in (1, -1):
+            self.send(self.first_ring(direction, 1, True))
+        for direction in (1, -1):
+            self.send(self.second_ring(0, direction, 1, True))
+
+    def first_arrival(self, hop):
+        half_way = (NZ if self.z_first else NY) // 2
+        for turn, direction in enumerate((1, -1)):
+            self.first_ring(direction, hop, False).wait_recv()
+            if hop < half_way:
+                self.send(self.first_ring(direction, hop + 1, True))
+                for across in (1, -1):
+                    self.send(self.second_ring(2 * hop - 1 + turn, across, 1, True))
+        if hop == half_way:
+            for across in (1, -1):
+                self.send(self.second_ring(2 * hop - 1, across, 1, True))
+
+    def second_arrival(self, block, hop):
+        half_way = (NY if self.z_first else NZ) // 2
+        for direction in (1, -1):
+            self.second_ring(block, direction, hop, False).wait_recv()
+            if hop < half_way:
+                self.send(self.second_ring(block, direction, hop + 1, True))
+
+    def stages(self):
+        blocks, ring, across = (NZ, NZ, NY) if self.z_first else (NY, NY, NZ)
+        out = [[self.begin]]
+        for hop in range(1, ring // 2 + 1):
+            out.append([functools.partial(self.first_arrival, hop)])
+        born = [0] + [(b + 1) // 2 for b in range(1, blocks)]
+        pace = 2 if self.z_first else 4
+        for b in range(blocks):
+            for hop in range(1, across // 2 + 1):
+                at = max(born[b] + hop, b * across * 3 // 2 // (2 * pace) + hop)
+                while len(out) <= at:
+                    out.append([])
+                out[at].append(functools.partial(self.second_arrival, b, hop))
+        return out
+
+    def finish(self):
+        for copy in self.sent:
+            copy.wait_send()
+
+
+def enter():
+    y, x, z = place()
+    barrier = pltpu.get_barrier_semaphore()
+    to = [(y, 1 - x, z), (y + 1, x, z), (y - 1, x, z), (y, x, z + 1), (y, x, z - 1)]
+    for t in to:
+        pl.semaphore_signal(barrier, inc=1, device_id={"ctx": ctx_of(*t)}, device_id_type=MESH)
+    pl.semaphore_wait(barrier, len(to))
+
+
+Q_A, O_A = 768, 640
+
+
+def gather_kernel(wq, wk, wv, wo, qa, qb, oa, ob, send_sems, recv_sems):
+    y, x, z = place()
+    qa[y, x, z] = wq[:, :Q_A]
+    rest = wq.shape[1] - Q_A
+    qb[y, x, z, :, :rest] = wq[:, Q_A:]
+    qb[y, x, z, :, rest : rest + HD] = wk[...]
+    qb[y, x, z, :, rest + HD :] = wv[...]
+    oa[y, x, z] = wo[:, :O_A]
+    ob[y, x, z] = wo[:, O_A:]
+    enter()
+    parts = []
+    first = 0
+    for buf, z_first in ((qa, True), (qb, False), (oa, True), (ob, False)):
+        parts.append(Gather(buf, send_sems, recv_sems, first, z_first))
+        first += COPIES_A if z_first else COPIES_B
+    for part in parts:
+        part.exchange()
+    plans = [part.stages() for part in parts]
+    lag = 5
+    for stage in range(lag + max(len(plan) for plan in plans)):
+        for index, plan in enumerate(plans):
+            at = stage - (lag if index >= 2 else 0)
+            if 0 <= at < len(plan):
+                for step in plan[at]:
+                    step()
+    for part in parts:
+        part.finish()
+
+
+def gather_weights(w_query, w_key, w_value, w_out_t):
+    rows = w_query.shape[0]
+    widths = [Q_A, w_query.shape[1] - Q_A + 2 * HD, O_A, w_out_t.shape[1] - O_A]
+    copies = 2 * (COPIES_A + COPIES_B)
+    return pl.pallas_call(
+        gather_kernel,
+        out_shape=[jax.ShapeDtypeStruct((NY, NX, NZ, rows, w), jnp.bfloat16) for w in widths],
+        in_specs=[pl.BlockSpec(memory_space=pltpu.VMEM)] * 4,
+        out_specs=[pl.BlockSpec(memory_space=pltpu.VMEM)] * 4,
+        scratch_shapes=[pltpu.SemaphoreType.DMA((copies,)), pltpu.SemaphoreType.DMA((copies,))],
+        compiler_params=pltpu.CompilerParams(
+            collective_id=0, has_side_effects=True, vmem_limit_bytes=48 * 1024 * 1024
+        ),
+    )(w_query, w_key, w_value, w_out_t)
 
 
 def passed_along(value, axis, steps):
@@ -69,21 +261,19 @@
     normed = (token_float * scale_inv * norm_gain).astype(jnp.bfloat16)
     context_rows = lax.all_gather(normed, "tp", axis=0, tiled=True)
     row_count = context_rows.shape[0]
-    query_sum = jnp.dot(
-        context_rows,
-        lax.all_gather(w_query, "ctx", axis=0, tiled=True),
-        preferred_element_type=jnp.float32,
-    )
-    key_sum = jnp.dot(
-        context_rows,
-        lax.all_gather(w_key, "ctx", axis=0, tiled=True),
-        preferred_element_type=jnp.float32,
-    )
-    value_sum = jnp.dot(
-        context_rows,
-        lax.all_gather(w_value, "ctx", axis=0, tiled=True),
-        preferred_element_type=jnp.float32,
-    )
+    qa, qb, oa, ob = gather_weights(w_query, w_key, w_value, w_out.T)
+    sums = [
+        jnp.dot(
+            context_rows,
+            w.reshape(-1, w.shape[-1]),
+            preferred_element_type=jnp.float32,
+        )
+        for w in (qa, qb)
+    ]
+    rest = w_query.shape[1] - Q_A
+    query_sum = jnp.concatenate([sums[0], sums[1][:, :rest]], axis=1)
+    key_sum = sums[1][:, rest : rest + HD]
+    value_sum = sums[1][:, rest + HD :]
     kv_local = w_key.shape[1] // HD
     group_size = w_query.shape[1] // w_key.shape[1]
     positions = ctx_index * row_count + jnp.arange(row_count, dtype=jnp.int32)
@@ -125,10 +315,11 @@
         .reshape(row_count, kv_local * group_size * HD)
         .astype(jnp.bfloat16)
     )
-    partial_out = jnp.dot(
-        attended,
-        lax.all_gather(w_out, "ctx", axis=1, tiled=True),
-        preferred_element_type=jnp.float32,
+    contract = (((1,), (1,)), ((), ()))
+    partial_out = lax.dot_general(
+        attended[:, :O_A], oa.reshape(-1, oa.shape[-1]), contract, preferred_element_type=jnp.float32
+    ) + lax.dot_general(
+        attended[:, O_A:], ob.reshape(-1, ob.shape[-1]), contract, preferred_element_type=jnp.float32
     )
     summed = lax.psum_scatter(
         partial_out.astype(jnp.bfloat16), "tp", scatter_dimension=0, tiled=True

time: 1340 us -> 328 us (0.24)
  waiting for transfers between devices: 1230 us -> 67 us
  Pallas kernels: 0 us -> 136 us
    all_gather x4 -> x0, waiting for transfers between devices: 1090 us -> none  [the longest x1 306 us: local(): lax.all_gather(w_query, 'ctx', axis=0, tiled=True)]
    pallas_call x0 -> x1, Pallas kernels: none -> 136 us  [gather_weights(): pl.pallas_call(gather_kernel, out_shape=[jax.ShapeDtypeStruct((NY, NX, NZ...]
    all_gather x1, waiting for transfers between devices: 52.2 us -> 0.01 us  [local(): context_rows = lax.all_gather(normed, 'tp', axis=0, tiled=True)]
  transfers between devices with their start and end apart: 9 -> 5, of which waited for: 9 -> 4; matrix products, arithmetic and copies ran while one was open for 6% -> 5% of each run, Pallas kernels for 0% -> 42%
where the time goes in v1:
time: 328 us; the launch traced here: 325 us
  Pallas kernels  136 us (41%)
  waiting for transfers between devices  67 us (20%)
  matrix products  45.7 us (14%)
  other arithmetic  32.5 us (10%)
  local copies, waits for them, and re-layouts  21.4 us (7%)
  between operations  13.7 us (4%)
  starting transfers between devices  8 us (2%)
    pallas_call x1, Pallas kernels, gather_weights(): pl.pallas_call(gather_kernel, out_shape=[jax.ShapeDtypeStruct((NY, NX, NZ...  136 us
    reduce_scatter x1, waiting for transfers between devices, local(): lax.psum_scatter(partial_out.astype(jnp.bfloat16), 'tp', scatter_dimensio...  56.8 us
    dot_general x4, matrix products, attend(): jnp.einsum('qkgs,skd->qkgd', weights, value_block, preferred_element_type...  13.3 us
    dot_general x2, matrix products, local(): jnp.dot(context_rows, w.reshape(-1, w.shape[-1]), preferred_element_type=...  13.1 us
    select_n x4, other arithmetic, doc_ranks(): return jnp.repeat(block_docs, BLOCK, total_repeat_length=per_device * BLOCK)  10.2 us
    ppermute x3, waiting for transfers between devices, passed_along(): lax.ppermute(value, axis, [(source, source + steps) for source in range(l...  10.2 us
    dot_general x4, matrix products, attend(): jnp.einsum('qkgd,skd->qkgs', query_heads, key_block, preferred_element_ty...  9.49 us
    ppermute x3, starting transfers between devices, passed_along(): lax.ppermute(value, axis, [(source, source + steps) for source in range(l...  7.92 us
  transfers between devices with their start and end apart: 5, of which 4 were waited for; matrix products, arithmetic and copies ran while one was open for 5% of the time, Pallas kernels for 42%

profile of v1, /device:TPU:38, one launch (start us, length us, event | category | flops | bytes accessed | tf_op | source)
XLA Modules:
  0.0 324.8 jit_solution(6345156325967503769)
XLA Ops:
  10.9 136.2 %shard_map.73 = (bf16[4,2,8,64,768]{4,3,2,1,0:T(8,128)(2,1)}, bf16[4,2,8,64,512]{4,3,2,1,0:T(8,128)(2,1)}, bf16[4,2,8,64,640]{4,3,2,1,0:T(8,128)(2,1)}, bf16[4,2,8,64,384]{4,3,2,1,0:T(8,128)(2,1)S(1)}) custom-call(bf16[64,1024]{1,0:T(8,128)(2,1)S(1)} %copy-done, bf16[64,128]{1,0:T(8,128)(2,1)S(1)} %copy-done.2, bf16[64,128]{1,0:T(8,128)(2,1)S(1)} %copy-done.3, ...), custom_call_target="tpu_custom_call" | custom-call | tf_op jit(solution)/shard_map/pallas_call | solution.py:195
  147.9 2.6 select_select_fusion.1
  152.5 5.8 %fusion.45 = f32[512,512]{0,1:T(8,128)S(1)} fusion(bf16[512,4096]{1,0:T(8,128)(2,1)} %all-gather.2.cloned.1.call-done, bf16[4096,512]{1,0:T(8,128)(2,1)} %bitcast.176), kind=kOutput, calls=%fused_computation.84 | convolution fusion | flops 2147483648 | bytes 9437184 | tf_op jit(solution)/shard_map/dot_general | solution.py:266
  162.7 7.3 %fusion.46 = f32[512,768]{1,0:T(8,128)S(1)} fusion(bf16[512,4096]{1,0:T(8,128)(2,1)} %all-gather.2.cloned.1.call-done, bf16[4096,768]{1,0:T(8,128)(2,1)} %bitcast.174), kind=kOutput, calls=%fused_computation.85 | convolution fusion | flops 3221225472 | bytes 12058624 | tf_op jit(solution)/shard_map/dot_general | solution.py:266
  176.9 4.8 %fusion.16 = f32[512,1,8,128]{0,3,2,1:T(8,128)} fusion(f32[512,8]{0,1:T(8,128)S(1)} %get-tuple-element.388, f32[512,512]{0,1:T(8,128)} %copy-done.12, f32[512,512,8]{1,0,2:T(8,128)S(1)} %get-tuple-element.398, f32[512,8]{0,1:T(8,128)S(1)} %get-tuple-element.390, pred[512,512]{0,1:T(8,128)(4,1)S(1)} %fusion.22), kind=kOutput, calls=%fused_computation.37 | convolution fusion | flops 545783808 | bytes 10911744 | tf_op jit(solution)/shard_map/qkgs,skd->qkgd/dot_general | solution.py:251
  181.7 2.9 copy.22
  186.4 3.8 %fusion.15 = bf16[512,1,8,128]{3,0,2,1:T(8,128)(2,1)} fusion(f32[512,1,8,64]{3,0,2,1:T(8,128)} %bitcast.163, f32[512,1,8,64]{3,0,2,1:T(8,128)} %bitcast.162), kind=kLoop, calls=%fused_computation.35 | loop fusion | flops 1572864 | bytes 3145728 | tf_op jit(solution)/shard_map/convert_element_type | solution.py:282
  190.2 56.4 %while.25 = (s32[]{:T(128)}, f32[512,1,8]{0,2,1:T(8,128)S(1)}, f32[512,1,8]{0,2,1:T(8,128)S(1)}, f32[512,1,8,128]{3,0,2,1:T(8,128)}, bf16[2,512,1,128]{3,1,2,0:T...) while((s32[]{:T(128)}, f32[512,1,8]{0,2,1:T(8,128)S(1)}, ...), condition=%wide.region_6.8_spmd, body=%wide.region_3.7_spmd.sunk | while | flops 1100238336 | bytes 50338176 | solution.py:311
  190.2 3.0 collective-permute-start
  194.0 2.5 select_select_fusion.3
  198.6 2.5 fusion.59
  203.7 2.8 bitcast_add_fusion.7
  207.9 3.0 collective-permute-start
  211.6 2.5 select_select_fusion.3
  214.4 3.2 collective-permute-done
  217.6 2.5 fusion.59
  222.6 2.8 bitcast_add_fusion.7
  232.2 5.1 %collective-permute-done = bf16[2,512,1,128]{3,1,2,0:T(8,128)(2,1)S(1)} collective-permute-done((bf16[2,512,1,128]{3,1,2,0:T(8,128)(2,1)}, bf16[2,512,1,128]{3,1,2,0:T(8,128)(2,1)S(1)}, u32[]{:S(2)}, u32[]{:S(2)}) %collective-permute-start) | collective-permute-done | bytes 262176 | tf_op jit(solution)/shard_map/while/body/eval_jaxpr/ppermute | solution.py:210
  237.3 2.6 fusion.59
  242.4 2.8 bitcast_add_fusion.7
  246.5 2.9 copy.24
  251.3 5.5 %fusion.23 = f32[512,4096]{1,0:T(8,128)S(1)} fusion(bf16[4096,640]{1,0:T(8,128)(2,1)} %bitcast.175, bf16[512,1024]{0,1:T(8,128)(2,1)S(1)} %bitcast.167), kind=kOutput, calls=%fused_computation.45 | convolution fusion | flops 2684354560 | bytes 14286848 | tf_op jit(solution)/shard_map/dot_general | solution.py:319
  256.8 4.4 %add_convert_fusion = bf16[512,4096]{1,0:T(8,128)(2,1)} fusion(f32[512,4096]{1,0:T(8,128)S(1)} %fusion.23, bf16[4096,384]{1,0:T(8,128)(2,1)S(1)} %bitcast.160, bf16[512,1024]{0,1:T(8,128)(2,1)S(1)} %bitcast.168), kind=kOutput, calls=%fused_computation.20 | convolution fusion | flops 1614807040 | bytes 16121856 | tf_op jit(solution)/shard_map/dot_general | solution.py:321
  261.2 56.8 %reduce-scatter.2.cloned.1.call-done = bf16[128,4096]{1,0:T(8,128)(2,1)} async-done(((bf16[512,4096]{1,0:T(8,128)(2,1)}), bf16[128,4096]{1,0:T(8,128)(2,1)}) %reduce-scatter.2.cloned.1.call-update) | async-done | bytes 1048592 | tf_op jit(solution)/shard_map/reduce_scatter | solution.py:324
  (95 shorter events, 42.4 us)
Async XLA Ops:
  6.5 4.3 %copy-start = (bf16[64,1024]{1,0:T(8,128)(2,1)S(1)}, bf16[64,1024]{1,0:T(8,128)(2,1)}, u32[]{:S(2)}) copy-start(bf16[64,1024]{1,0:T(8,128)(2,1)} %wq.1) | copy-start | bytes 393220
  6.5 4.3 %copy-start.2 = (bf16[64,128]{1,0:T(8,128)(2,1)S(1)}, bf16[64,128]{1,0:T(8,128)(2,1)}, u32[]{:S(2)}) copy-start(bf16[64,128]{1,0:T(8,128)(2,1)} %wk.1) | copy-start | bytes 49156
  6.5 4.3 %copy-start.3 = (bf16[64,128]{1,0:T(8,128)(2,1)S(1)}, bf16[64,128]{1,0:T(8,128)(2,1)}, u32[]{:S(2)}) copy-start(bf16[64,128]{1,0:T(8,128)(2,1)} %wv.1) | copy-start | bytes 49156
  6.5 4.3 %copy-start.1 = (bf16[1024,64]{0,1:T(8,128)(2,1)S(1)}, bf16[1024,64]{0,1:T(8,128)(2,1)}, u32[]{:S(2)}) copy-start(bf16[1024,64]{0,1:T(8,128)(2,1)} %param.20) | copy-start | bytes 393220
  6.5 140.6 %copy-start.14 = (s32[256]{0:T(256)S(1)}, s32[256]{0:T(256)}, u32[]{:S(2)}) copy-start(s32[256]{0:T(256)} %param.21) | copy-start | bytes 3076
  6.5 146.0 %all-gather.2.cloned.1.call-start = ((), (), s32[]{:S(2)}) async-start(), calls=%async_computation.1 | async-start | bytes 5242880 | tf_op jit(solution)/shard_map/all_gather | solution.py:262
  10.8 307.2 %reduce-scatter.2.cloned.1.call-start = ((), (), s32[]{:S(2)}) async-start(), calls=%async_computation.2 | async-start | bytes 5242880 | tf_op jit(solution)/shard_map/reduce_scatter | solution.py:324
  158.3 1.6 copy-start.12
  162.7 7.3 %copy-start.8 = (f32[512,256]{1,0:T(8,128)S(1)}, f32[512,256]{1,0:T(8,128)}, u32[]{:S(2)}) copy-start(f32[512,256]{1,0:T(8,128)} %copy.17) | copy-start | bytes 1572868
  170.8 1.0 copy-start.11
  170.8 1.5 copy-start.9
  170.8 1.5 copy-start.10
  172.3 0.8 copy-start.13
  173.1 1.9 copy-start.4
  173.1 2.0 copy-start.5
  190.2 8.5 %collective-permute-start = (bf16[2,512,1,128]{3,1,2,0:T(8,128)(2,1)}, bf16[2,512,1,128]{3,1,2,0:T(8,128)(2,1)S(1)}, u32[]{:S(2)}, u32[]{:S(2)}) collective-permute-start(bf16[2,512,1,128]{3,1,2,0:T(8,128)(2,1)} %get-tuple-element.487), channel_id=1, source_target_pairs={{0,4},{4,8},{8,12},{12,16},{16,20},{20,24},{24,28},{28,32},{32,36}... | collective-permute-start | bytes 786440 | tf_op jit(solution)/shard_map/while/body/eval_jaxpr/ppermute | solution.py:210
  201.2 2.5 copy-start.6
  206.5 1.3 copy-start.7
  207.9 9.7 %collective-permute-start = (bf16[2,512,1,128]{3,1,2,0:T(8,128)(2,1)}, bf16[2,512,1,128]{3,1,2,0:T(8,128)(2,1)S(1)}, u32[]{:S(2)}, u32[]{:S(2)}) collective-permute-start(bf16[2,512,1,128]{3,1,2,0:T(8,128)(2,1)} %get-tuple-element.487), channel_id=1, source_target_pairs={{0,4},{4,8},{8,12},{12,16},{16,20},{20,24},{24,28},{28,32},{32,36}... | collective-permute-start | bytes 786440 | tf_op jit(solution)/shard_map/while/body/eval_jaxpr/ppermute | solution.py:210
  220.1 2.5 copy-start.6
  225.4 1.3 copy-start.7
  226.8 10.6 %collective-permute-start = (bf16[2,512,1,128]{3,1,2,0:T(8,128)(2,1)}, bf16[2,512,1,128]{3,1,2,0:T(8,128)(2,1)S(1)}, u32[]{:S(2)}, u32[]{:S(2)}) collective-permute-start(bf16[2,512,1,128]{3,1,2,0:T(8,128)(2,1)} %get-tuple-element.487), channel_id=1, source_target_pairs={{0,4},{4,8},{8,12},{12,16},{16,20},{20,24},{24,28},{28,32},{32,36}... | collective-permute-start | bytes 786440 | tf_op jit(solution)/shard_map/while/body/eval_jaxpr/ppermute | solution.py:210
  239.9 2.5 copy-start.6
  245.2 1.3 copy-start.7
Sparse Core Ops, SparseCore 0:
  10.9 42.0 all-gather.1
  261.3 56.5 reduce-scatter.1

commit v2 on v0

v2 whole, which is shorter than its diff:
```python
import functools

import jax
import jax.numpy as jnp
from jax import lax
from jax.experimental import pallas as pl
from jax.experimental.pallas import tpu as pltpu
from jax.sharding import PartitionSpec as P

HD = 128
BLOCK = 128
WINDOW = 12
SPAN = 4
NY, NX, NZ, NTP = 4, 2, 8, 4
RING_X = 4
MESH = pl.DeviceIdType.MESH

rope_base = 500000.0
neg_large = -1e30

Z_OFFSETS = [0, -1, 1, -2, 2, -3, 3, 4]
Y_OFFSETS = [0, -1, 1, 2]
COPIES_A = 8 + 32
COPIES_B = 4 + 32
Q_A = 384
O_A = 384
NT = (((1,), (1,)), ((), ()))


class Place:
    def __init__(self):
        c, t = lax.axis_index("ctx"), lax.axis_index("tp")
        self.y, self.xl, self.z = c // (NX * NZ), lax.rem(c // NZ, NX), lax.rem(c, NZ)
        self.xh, self.core = t // 2, lax.rem(t, 2)
        self.x = self.xh * 2 + self.xl


def device(y, x, z, core):
    x = lax.rem(x + RING_X, RING_X)
    ctx = (lax.rem(y + NY, NY) * NX + lax.rem(x, 2)) * NZ + lax.rem(z + NZ, NZ)
    return (ctx, (x // 2) * 2 + core)


class Copies:
    def __init__(self, send_sems, recv_sems):
        self.send_sems, self.recv_sems = send_sems, recv_sems
        self.used = 0
        self.sent = []

    def reserve(self, count):
        first = self.used
        self.used += count
        return first

    def make(self, index, src, dst, to, recv_index=None):
        return pltpu.make_async_remote_copy(
            src_ref=src,
            dst_ref=dst,
            send_sem=self.send_sems.at[index],
            recv_sem=self.recv_sems.at[index if recv_index is None else recv_index],
            device_id=to,
            device_id_type=MESH,
        )

    def send(self, copy, when=None):
        if when is None:
            copy.start()
        else:
            pl.when(when)(copy.start)
        self.sent.append((copy, when))

    def finish(self):
        for copy, when in self.sent:
            if when is None:
                copy.wait_send()
            else:
                pl.when(when)(copy.wait_send)


class Gather:
    def __init__(self, here, copies, buf, z_first):
        self.here, self.copies, self.buf, self.z_first = here, copies, buf, z_first
        self.first = copies.reserve(COPIES_A if z_first else COPIES_B)
        self.arrive = copies.reserve(2)

    def exchange(self, parts):
        h = self.here
        for p in (0, 1):
            local = jnp.logical_and(h.core == h.xl, h.core == p)

            @pl.when(local)
            def _():
                self.buf[h.y, h.xl, h.z] = parts[p][...]

            copy = self.copies.make(
                self.arrive + p,
                parts[p],
                self.buf.at[h.y, h.xl, h.z],
                device(h.y, h.xh * 2 + h.core, h.z, p),
                self.arrive + h.xl,
            )
            self.copies.send(copy, jnp.logical_not(local))

    def exchanged(self):
        h = self.here
        for slot in (0, 1):
            local = jnp.logical_and(h.core == h.xl, h.xl == slot)
            ref = self.buf.at[h.y, slot, h.z]
            copy = self.copies.make(self.arrive + slot, ref, ref, device(h.y, h.x + 1, h.z, h.core))
            pl.when(jnp.logical_not(local))(copy.wait_recv)

    def copy(self, index, yy, zz, half, to):
        yy, zz = lax.rem(yy + 2 * NY, NY), lax.rem(zz + 2 * NZ, NZ)
        ref = self.buf.at[yy, :, zz] if half is None else self.buf.at[yy, half, zz]
        return self.copies.make(self.first + index, ref, ref, to)

    def ring_id(self, second, block, direction, hop, length):
        base = 0 if not second else (NZ if self.z_first else NY) + block * length
        return base + (0 if direction > 0 else length // 2) + hop - 1

    def along_z(self, second, y_offset, block, direction, hop, sending):
        h = self.here
        distance = hop - 1 if sending else hop
        half = (0 if direction > 0 else 1) if hop == NZ // 2 else None
        return self.copy(
            self.ring_id(second, block, direction, hop, NZ),
            h.y + y_offset,
            h.z - direction * distance,
            half,
            device(h.y, h.x, h.z + direction, h.core),
        )

    def along_y(self, second, z_offset, block, direction, hop, sending):
        h = self.here
        distance = hop - 1 if sending else hop
        half = (0 if direction > 0 else 1) if hop == NY // 2 else None
        return self.copy(
            self.ring_id(second, block, direction, hop, NY),
            h.y - direction * distance,
            h.z + z_offset,
            half,
            device(h.y + direction, h.x, h.z, h.core),
        )

    def first_ring(self, direction, hop, sending):
        along = self.along_z if self.z_first else self.along_y
        return along(False, 0, 0, direction, hop, sending)

    def second_ring(self, block, direction, hop, sending):
        if self.z_first:
            return self.along_y(True, Z_OFFSETS[block], block, direction, hop, sending)
        return self.along_z(True, Y_OFFSETS[block], block, direction, hop, sending)

    def begin(self):
        self.exchanged()
        for direction in (1, -1):
            self.copies.send(self.first_ring(direction, 1, True))
        for direction in (1, -1):
            self.copies.send(self.second_ring(0, direction, 1, True))

    def first_arrival(self, hop):
        half_way = (NZ if self.z_first else NY) // 2
        for turn, direction in enumerate((1, -1)):
            self.first_ring(direction, hop, False).wait_recv()
            if hop < half_way:
                self.copies.send(self.first_ring(direction, hop + 1, True))
                for across in (1, -1):
                    self.copies.send(self.second_ring(2 * hop - 1 + turn, across, 1, True))
        if hop == half_way:
            for across in (1, -1):
                self.copies.send(self.second_ring(2 * hop - 1, across, 1, True))

    def second_arrival(self, block, hop):
        half_way = (NY if self.z_first else NZ) // 2
        for direction in (1, -1):
            self.second_ring(block, direction, hop, False).wait_recv()
            if hop < half_way:
                self.copies.send(self.second_ring(block, direction, hop + 1, True))

    def stages(self):
        blocks, ring, across = (NZ, NZ, NY) if self.z_first else (NY, NY, NZ)
        out = [[self.begin]]
        for hop in range(1, ring // 2 + 1):
            out.append([functools.partial(self.first_arrival, hop)])
        born = [0] + [(b + 1) // 2 for b in range(1, blocks)]
        pace = 2 if self.z_first else 4
        for b in range(blocks):
            for hop in range(1, across // 2 + 1):
                at = max(born[b] + hop, b * across * 3 // 2 // (2 * pace) + hop)
                while len(out) <= at:
                    out.append([])
                out[at].append(functools.partial(self.second_arrival, b, hop))
        return out


class Tokens:
    def __init__(self, here, copies, rows):
        self.here, self.copies, self.rows = here, copies, rows
        self.first = copies.reserve(13)

    def part(self, x, core, half):
        x = lax.rem(x + RING_X, RING_X)
        ref = self.rows.at[lax.rem(x, 2), (x // 2) * 2 + core]
        return ref if half is None else ref.at[pl.ds(half * (BLOCK // 2), BLOCK // 2)]

    def ring(self, direction, hop, half, sending):
        h = self.here
        index = (0 if direction > 0 else 2) + half if hop == 1 else 4 + half
        ref = self.part(h.x - direction * (hop - 1 if sending else hop), h.core, half)
        return self.copies.make(self.first + index, ref, ref, device(h.y, h.x + direction, h.z, h.core))

    def beside(self, distance, half, sending):
        h = self.here
        index = 6 if half is None else {-1: 7, 1: 9, 2: 11}[distance] + half
        ref = self.part(h.x + distance, h.core if sending else 1 - h.core, half)
        return self.copies.make(self.first + index, ref, ref, device(h.y, h.x, h.z, 1 - h.core))

    def begin(self):
        for turn in (0, 1):
            self.copies.send(self.ring(1, 1, turn, True))
            self.copies.send(self.ring(-1, 1, 1 - turn, True))
        self.copies.send(self.beside(0, None, True))

    def first_hop(self, turn):
        for direction in (1, -1):
            half = turn if direction > 0 else 1 - turn
            self.ring(direction, 1, half, False).wait_recv()
            if turn == 0:
                self.copies.send(self.ring(direction, 2, half, True))
            self.copies.send(self.beside(-direction, half, True))

    def second_hop(self):
        for direction, half in ((1, 0), (-1, 1)):
            self.ring(direction, 2, half, False).wait_recv()
            self.copies.send(self.beside(2, half, True))

    def rest(self):
        self.beside(0, None, False).wait_recv()
        for distance in (-1, 1, 2):
            for half in (0, 1):
                self.beside(distance, half, False).wait_recv()


class Relay:
    def __init__(self, here, copies, kv, hops):
        self.here, self.copies, self.kv, self.hops = here, copies, kv, hops
        self.first = copies.reserve(10)

    def slot(self, kind, distance, xl=None):
        rows = pl.ds((SPAN - 1 - distance) * self.rows(), self.rows())
        return self.kv.at[kind, :, rows] if xl is None else self.kv.at[kind, xl, rows]

    def rows(self):
        return self.kv.shape[2] // SPAN

    def along(self, distance):
        h = self.here
        src = self.slot(h.core, 0) if distance == 1 else self.hops.at[distance - 2]
        return self.copies.make(
            self.first + distance - 1,
            src,
            self.hops.at[distance - 1],
            device(h.y, h.x, h.z + 1, h.core),
        )

    def over(self, distance):
        h = self.here
        return self.copies.make(
            self.first + 2 + distance,
            self.hops.at[distance - 1, 1],
            self.slot(h.core, distance, 0),
            device(h.y + 1, h.x, h.z, h.core),
        )

    def beside(self, distance, sending):
        h = self.here
        ref = self.slot(h.core if sending else 1 - h.core, distance)
        return self.copies.make(self.first + 6 + distance, ref, ref, device(h.y, h.x, h.z, 1 - h.core))

    def begin(self):
        self.copies.send(self.along(1))
        self.copies.send(self.beside(0, True))

    def arrival(self, distance):
        h = self.here
        self.along(distance).wait_recv()
        if distance < SPAN - 1:
            self.copies.send(self.along(distance + 1))
        wrapped = h.z < distance
        start = (SPAN - 1 - distance) * self.rows()
        rows = pl.ds(start, self.rows())
        self.copies.send(self.over(distance), wrapped)

        @pl.when(wrapped)
        def _():
            self.kv[h.core, 1, rows] = self.hops[distance - 1, 0]

        @pl.when(jnp.logical_not(wrapped))
        def _():
            self.kv[h.core, 0, rows] = self.hops[distance - 1, 0]
            self.kv[h.core, 1, rows] = self.hops[distance - 1, 1]

    def placed(self, distance):
        pl.when(self.here.z < distance)(self.over(distance).wait_recv)
        self.copies.send(self.beside(distance, True))

    def rest(self):
        for distance in range(SPAN):
            self.beside(distance, False).wait_recv()


class Products:
    def __init__(self, here, copies, own, other, part_a, part_b, whole_a, whole_b):
        self.here, self.copies, self.own, self.other = here, copies, own, other
        self.half_way = {1: part_a, -1: part_b}
        self.whole = {1: whole_a, -1: whole_b}
        self.first = copies.reserve(10)
        self.width = own.shape[-1] // 2

    def columns(self, half):
        return pl.ds(half * self.width, self.width)

    def beside(self, j):
        h = self.here
        return self.copies.make(
            self.first + j,
            self.own.at[1 - h.core, j],
            self.other.at[j],
            device(h.y, h.x, h.z, 1 - h.core),
        )

    def far(self, direction):
        h = self.here
        half = 0 if direction > 0 else 1
        return self.copies.make(
            self.first + 4 + half,
            self.own.at[h.core, 0, :, self.columns(half)],
            self.half_way[direction],
            device(h.y, h.x + direction, h.z, h.core),
        )

    def near(self, direction, half):
        h = self.here
        j = 1 if direction > 0 else 2
        return self.copies.make(
            self.first + 6 + 2 * (j - 1) + half,
            self.own.at[h.core, j, :, self.columns(half)],
            self.whole[direction].at[:, self.columns(half)],
            device(h.y, h.x + direction, h.z, h.core),
        )

    def add(self, j, half, more=None):
        h = self.here
        tile = 512

        def body(step, _):
            inner = pl.multiple_of(step * tile, tile)
            at = pl.ds(pl.multiple_of(half * self.width + inner, tile), tile)
            total = self.own[h.core, j, :, at].astype(jnp.float32) + self.other[j, :, at].astype(jnp.float32)
            if more is not None:
                total = total + more[:, pl.ds(inner, tile)].astype(jnp.float32)
            self.own[h.core, j, :, at] = total.astype(jnp.bfloat16)
            return 0

        lax.fori_loop(0, self.width // tile, body, 0)

    def reduce(self, j):
        self.beside(j).wait_recv()
        if j == 0:
            for direction in (1, -1):
                self.add(0, 0 if direction > 0 else 1)
                self.copies.send(self.far(direction))
        elif j < 3:
            direction = 1 if j == 1 else -1
            half = 1 if direction > 0 else 0
            self.add(j, half)
            self.copies.send(self.near(direction, half))

    def last(self, out):
        h = self.here
        for direction in (1, -1):
            j, half = (1, 0) if direction > 0 else (2, 1)
            self.far(direction).wait_recv()
            self.add(j, half, self.half_way[direction])
            self.copies.send(self.near(direction, half))
        for half in (0, 1):
            for direction in (1, -1):
                self.near(direction, half).wait_recv()
        tile = 512

        def body(step, _):
            at = pl.ds(pl.multiple_of(step * tile, tile), tile)
            total = self.own[h.core, 3, :, at].astype(jnp.float32) + self.other[3, :, at].astype(jnp.float32)
            for direction in (1, -1):
                total = total + self.whole[direction][:, at].astype(jnp.float32)
            out[:, at] = total.astype(out.dtype)
            return 0

        lax.fori_loop(0, 2 * self.width // tile, body, 0)


def neighbours(h):
    outer = h.x - 1 + 2 * h.xl
    return [
        device(h.y, h.x, h.z, 1 - h.core),
        device(h.y, h.xh * 2 + 1 - h.xl, h.z, h.core),
        device(h.y, h.xh * 2 + 1 - h.xl, h.z, 1 - h.core),
        device(h.y, outer, h.z, h.core),
        device(h.y + 1, h.x, h.z, h.core),
        device(h.y - 1, h.x, h.z, h.core),
        device(h.y, h.x, h.z + 1, h.core),
        device(h.y, h.x, h.z - 1, h.core),
    ]


def block_kernel(
    tokens, gain, wq, wk, wv, wo, cosine, sine, bias, out,
    rows, qa, qb, qb_own, oa, ob, queries, kv, values, hops, attended,
    own, other, part_a, part_b, whole_a, whole_b, send_sems, recv_sems,
):
    h = Place()
    half_heads = wq.shape[1] // 2
    barrier = pltpu.get_barrier_semaphore()
    greeted = neighbours(h)
    for to in greeted:
        pl.semaphore_signal(barrier, inc=1, device_id=to, device_id_type=MESH)

    for p, kind in ((0, wk), (1, wv)):
        qb_own[p, :, :HD] = wq[:, p * half_heads + Q_A : (p + 1) * half_heads]
        qb_own[p, :, HD:] = kind[...]

    def norm(step, _):
        at = pl.ds(pl.multiple_of(step * 32, 32), 32)
        value = tokens[at, :].astype(jnp.float32)
        scale = lax.rsqrt(jnp.mean(value * value, axis=-1, keepdims=True) + 1e-05)
        rows[h.xl, h.xh * 2 + h.core, at, :] = (value * scale * gain[...]).astype(jnp.bfloat16)
        return 0

    lax.fori_loop(0, BLOCK // 32, norm, 0)
    pl.semaphore_wait(barrier, len(greeted))

    copies = Copies(send_sems, recv_sems)
    gathers = [Gather(h, copies, buf, z_first) for buf, z_first in ((qa, True), (qb, False), (oa, True), (ob, False))]
    token_rows = Tokens(h, copies, rows)
    relay = Relay(h, copies, kv, hops)
    products = Products(h, copies, own, other, part_a, part_b, whole_a, whole_b)

    gathers[0].exchange([wq.at[:, pl.ds(p * half_heads, Q_A)] for p in (0, 1)])
    gathers[1].exchange([qb_own.at[p] for p in (0, 1)])
    token_rows.begin()
    gathers[2].exchange([wo.at[:, pl.ds(p * half_heads, O_A)] for p in (0, 1)])
    gathers[3].exchange([wo.at[:, pl.ds(p * half_heads + O_A, half_heads - O_A)] for p in (0, 1)])

    plans = [part.stages() for part in gathers]

    def run(which, stage):
        for index in which:
            if 0 <= stage < len(plans[index]):
                for step in plans[index][stage]:
                    step()

    first_stages = max(len(plans[0]), len(plans[1]))
    last_stages = max(len(plans[2]), len(plans[3]))
    early = 3
    for stage in range(first_stages):
        run((0, 1), stage)
        run((2, 3), stage - (first_stages - early))
        if stage == 4:
            token_rows.first_hop(0)
        if stage == first_stages - 2:
            token_rows.first_hop(1)
    token_rows.second_hop()
    token_rows.rest()

    def project(weights, chip):
        at = pl.ds((chip // 2) * 2, 2)
        total = None
        depth = NX * NZ * weights.shape[3]
        for y in range(NY):
            left = rows[lax.rem(chip, 2), at, :, y * depth : (y + 1) * depth].reshape(2 * BLOCK, depth)
            term = jnp.dot(left, weights[y].reshape(depth, weights.shape[4]), preferred_element_type=jnp.float32)
            total = term if total is None else total + term
        return total

    def rotated(value, chip):
        at = pl.ds(pl.multiple_of((chip // 2) * (2 * BLOCK), 2 * BLOCK), 2 * BLOCK)
        swapped = pltpu.roll(value, HD // 2, 1)
        return value * cosine[lax.rem(chip, 2), at, :] + swapped * sine[lax.rem(chip, 2), at, :]

    def keep_query(value, chip, head):
        query = (rotated(value, chip) * HD ** (-0.5)).astype(jnp.bfloat16)
        for core in (0, 1):
            queries[lax.rem(chip, 2), (chip // 2) * 2 + core, head * BLOCK : (head + 1) * BLOCK, :] = query[
                core * BLOCK : (core + 1) * BLOCK
            ]

    def project_b(chip, _):
        total = project(qb, chip)
        keep_query(total[:, :HD], chip, 3)
        value = total[:, HD:]
        value = jnp.where(h.core == 0, rotated(value, chip), value).astype(jnp.bfloat16)
        start = (SPAN - 1) * NTP * BLOCK + (chip // 2) * (2 * BLOCK)
        kv[h.core, lax.rem(chip, 2), pl.ds(pl.multiple_of(start, 2 * BLOCK), 2 * BLOCK), :] = value
        return 0

    def project_a(chip, _):
        total = project(qa, chip)
        for head in range(3):
            keep_query(total[:, head * HD : (head + 1) * HD], chip, head)
        return 0

    lax.fori_loop(0, RING_X, project_b, 0)
    relay.begin()
    run((2, 3), early)
    lax.fori_loop(0, RING_X, project_a, 0)
    stage = early + 1
    for distance in range(1, SPAN):
        relay.arrival(distance)
        run((2, 3), stage)
        stage += 1
        relay.placed(distance)
    for stage in range(stage, last_stages):
        run((2, 3), stage)
    relay.rest()

    values[:, :, HD:] = jnp.ones_like(values[:, :, HD:])
    for xl in range(NX):
        values[xl, :, :HD] = kv[1, xl]

    heads = half_heads // HD
    query_at = lax.broadcasted_iota(jnp.int32, (2 * BLOCK, BLOCK), 0)
    query_at = lax.rem(query_at, BLOCK)
    causal = jnp.where(query_at >= lax.broadcasted_iota(jnp.int32, (2 * BLOCK, BLOCK), 1), 0.0, neg_large)

    def attend(chip):
        xl, first_block = lax.rem(chip, 2), (chip // 2) * 2

        def body(step, _):
            block = first_block + step
            window = pl.ds(pl.multiple_of((block + SPAN * NTP - WINDOW - (NTP - 1)) * BLOCK, BLOCK), WINDOW * BLOCK)
            for pair in range(heads // 2):
                query = queries[xl, block, pair * 2 * BLOCK : (pair + 1) * 2 * BLOCK, :]
                scores = lax.dot_general(query, kv[0, xl, window, :], NT, preferred_element_type=jnp.float32)
                scores = scores + bias[xl * NTP + block]
                near = (WINDOW - 1) * BLOCK
                scores = jnp.concatenate([scores[:, :near], scores[:, near:] + causal], axis=1)
                top = jnp.max(scores, axis=-1, keepdims=True)
                weights = jnp.exp(scores - top).astype(jnp.bfloat16)
                total = jnp.dot(weights, values[xl, window, :], preferred_element_type=jnp.float32)
                result = (total[:, :HD] / total[:, HD:]).astype(jnp.bfloat16)
                for k in range(2):
                    head = pair * 2 + k
                    attended[xl, block, :, head * HD : (head + 1) * HD] = result[k * BLOCK : (k + 1) * BLOCK]
            return 0

        lax.fori_loop(0, 2, body, 0)

    def multiply(j, chip):
        xl, first_block = lax.rem(chip, 2), (chip // 2) * 2
        tile = NZ * wo.shape[0]

        def body(step, _):
            left = attended[xl, pl.ds(first_block, 2)].reshape(2 * BLOCK, half_heads)
            y, x = step // NX, lax.rem(step, NX)
            right = jnp.concatenate(
                [oa[y, x].reshape(tile, O_A), ob[y, x].reshape(tile, half_heads - O_A)], axis=1
            )
            total = lax.dot_general(left, right, NT, preferred_element_type=jnp.float32).astype(jnp.bfloat16)
            at = pl.ds(pl.multiple_of(step * tile, tile), tile)
            for core in (0, 1):
                own[core, j, :, at] = total[core * BLOCK : (core + 1) * BLOCK]
            return 0

        lax.fori_loop(0, NY * NX, body, 0)

    for j, offset in enumerate((2, 1, 3, 0)):
        chip = lax.rem(h.x + offset, RING_X)
        attend(chip)
        if j > 0:
            products.reduce(j - 1)
        multiply(j, chip)
        copies.send(products.beside(j))
    products.reduce(3)
    products.last(out)
    copies.finish()


COPIES = 2 * (COPIES_A + COPIES_B + 4) + 13 + 10 + 10


def whole_block(tokens, gain, w_query, w_key, w_value, w_out_t, cosine, sine, bias):
    count, width = tokens.shape
    rows = w_query.shape[0]
    half = w_query.shape[1] // 2
    near = NTP * count
    bf16 = jnp.bfloat16
    vmem = pl.BlockSpec(memory_space=pltpu.VMEM)
    return pl.pallas_call(
        block_kernel,
        out_shape=jax.ShapeDtypeStruct((count, width), bf16),
        in_specs=[vmem] * 9,
        out_specs=vmem,
        scratch_shapes=[
            pltpu.VMEM((NX, NTP, count, width), bf16),
            pltpu.VMEM((NY, NX, NZ, rows, Q_A), bf16),
            pltpu.VMEM((NY, NX, NZ, rows, half - Q_A + HD), bf16),
            pltpu.VMEM((2, rows, half - Q_A + HD), bf16),
            pltpu.VMEM((NY, NX, NZ, rows, O_A), bf16),
            pltpu.VMEM((NY, NX, NZ, rows, half - O_A), bf16),
            pltpu.VMEM((NX, NTP, half // HD * BLOCK, HD), bf16),
            pltpu.VMEM((2, NX, SPAN * near, HD), bf16),
            pltpu.VMEM((NX, SPAN * near, 2 * HD), bf16),
            pltpu.VMEM((SPAN - 1, NX, near, HD), bf16),
            pltpu.VMEM((NX, NTP, count, half), bf16),
            pltpu.VMEM((2, RING_X, count, width), bf16),
            pltpu.VMEM((RING_X, count, width), bf16),
            pltpu.VMEM((count, width // 2), bf16),
            pltpu.VMEM((count, width // 2), bf16),
            pltpu.VMEM((count, width), bf16),
            pltpu.VMEM((count, width), bf16),
            pltpu.SemaphoreType.DMA((COPIES,)),
            pltpu.SemaphoreType.DMA((COPIES,)),
        ],
        compiler_params=pltpu.CompilerParams(
            collective_id=0, has_side_effects=True, vmem_limit_bytes=60 * 1024 * 1024
        ),
    )(tokens, gain, w_query, w_key, w_value, w_out_t, cosine, sine, bias)


def tables(doc_blocks, count):
    c = lax.axis_index("ctx")
    y, z = c // (NX * NZ), lax.rem(c, NZ)
    contexts = y * (NX * NZ) + jnp.arange(NX, dtype=jnp.int32) * NZ + z
    positions = contexts[:, None] * (NTP * count) + jnp.arange(NTP * count, dtype=jnp.int32)[None, :]
    half_width = HD // 2
    frequency = rope_base ** (-jnp.arange(half_width, dtype=jnp.float32) / half_width)
    angles = positions.astype(jnp.float32)[..., None] * frequency
    cosine, sine = jnp.cos(angles), jnp.sin(angles)
    cosine = jnp.concatenate([cosine, cosine], axis=-1)
    sine = jnp.concatenate([-sine, sine], axis=-1)
    blocks = (contexts[:, None] * NTP + jnp.arange(NTP, dtype=jnp.int32)).reshape(-1)
    keys = blocks[:, None] - (WINDOW - 1) + jnp.arange(WINDOW, dtype=jnp.int32)
    visible = (keys >= 0) & (doc_blocks[jnp.maximum(keys, 0)] == doc_blocks[blocks][:, None])
    bias = jnp.where(visible, 0.0, neg_large).astype(jnp.float32)
    bias = jnp.broadcast_to(bias[:, None, :, None], (NX * NTP, 1, WINDOW, BLOCK)).reshape(NX * NTP, 1, WINDOW * BLOCK)
    return cosine, sine, bias


def local(tokens, norm_gain, w_query, w_key, w_value, w_out, doc_blocks):
    cosine, sine, bias = tables(doc_blocks, tokens.shape[0])
    return whole_block(tokens, norm_gain[None, :], w_query, w_key, w_value, w_out.T, cosine, sine, bias)


def solution(mesh):
    return jax.shard_map(
        local,
        mesh=mesh,
        in_specs=(
            P(("ctx", "tp"), None),
            P(),
            P("ctx", "tp"),
            P("ctx", "tp"),
            P("ctx", "tp"),
            P("tp", "ctx"),
            P(),
        ),
        out_specs=P(("ctx", "tp"), None),
        check_vma=False,
    )
```

time: 1340 us -> 174 us (0.13)
  waiting for transfers between devices: 1230 us -> 0 us
  Pallas kernels: 0 us -> 164 us
  matrix products: 43.7 us -> 0 us
  other arithmetic: 31.7 us -> 4.24 us
  between operations: 13.7 us -> 0.04 us
    all_gather x5 -> x0, waiting for transfers between devices: 1140 us -> none  [the longest x1 306 us: local(): lax.all_gather(w_query, 'ctx', axis=0, tiled=True)]
    pallas_call x0 -> x1, Pallas kernels: none -> 164 us  [whole_block(): pl.pallas_call(block_kernel, out_shape=jax.ShapeDtypeStruct((count, width...]
    reduce_scatter x1 -> x0, waiting for transfers between devices: 65.9 us -> none  [local(): lax.psum_scatter(partial_out.astype(jnp.bfloat16), 'tp', scatter_dimensio...]
    dot_general x12 -> x0, matrix products: 43.7 us -> none  [the longest x4 12.1 us: attend(): jnp.einsum('qkgs,skd->qkgd', weights, value_block, preferred_element_type...]
    ppermute x3 -> x0, waiting for transfers between devices: 18.6 us -> none  [passed_along(): lax.ppermute(value, axis, [(source, source + steps) for source in range(l...]
  transfers between devices with their start and end apart: 9 -> 0, of which waited for: 9 -> 0; matrix products, arithmetic and copies ran while one was open for 6% -> 0% of each run, Pallas kernels for 0% -> 0%
where the time goes in v2:
time: 174 us
  Pallas kernels  164 us (94%)
  local copies, waits for them, and re-layouts  5.77 us (3%)
  other arithmetic  4.24 us (2%)
    pallas_call x1, Pallas kernels, whole_block(): pl.pallas_call(block_kernel, out_shape=jax.ShapeDtypeStruct((count, width...  164 us

profile of v2, /device:TPU:38, one launch (start us, length us, event | category | flops | bytes accessed | tf_op | source)
XLA Modules:
  0.0 173.9 jit_solution(12508729003469358570)
XLA Ops:
  0.0 0.0 copy-start
  0.0 0.1 iota_add_fusion
  0.1 0.1 add.138
  0.2 0.1 sub.11
  0.3 0.4 copy-done
  0.7 0.6 gather_fusion.1
  1.3 0.1 add_maximum_fusion
  1.4 0.1 reshape.164
  1.5 1.3 gather_fusion
  2.8 0.1 reshape.163
  2.8 0.1 fusion.2
  2.9 0.1 copy.8
  3.0 0.1 add_convert_fusion
  3.1 0.1 broadcast_bitcast_fusion
  3.2 0.7 copy.9.bias
  3.8 1.9 %fusion = (f32[2,512,64]{2,1,0:T(8,128)S(1)}, f32[2,512,64]{2,1,0:T(8,128)S(1)}, f32[2,512,64]{2,1,0:T(8,128)S(1)}) fusion(f32[64]{0:T(128)S(1)} %multiply_power_fusion, f32[2,512]{1,0:T(2,128)S(1)} %add_convert_fusion), kind=kLoop, calls=%fused_computation.6 | loop fusion | flops 131072 | bytes 790784 | tf_op jit(solution)/shard_map/neg | solution.py:640
  5.7 1.0 pad_maximum_fusion.1.sine
  6.8 1.0 pad_maximum_fusion.cosine
  7.8 163.9 %shard_map.73 = bf16[128,4096]{1,0:T(8,128)(2,1)} custom-call(bf16[128,4096]{1,0:T(8,128)(2,1)} %tokens.1, f32[1,4096]{1,0:T(1,128)} %bitcast.9, bf16[64,1024]{1,0:T(8,128)(2,1)} %wq.1, bf16[64,128]{1,0:T(8,128)(2,1)} %wk.1, bf16[64,128]{1,0:T(8,128)(2,1)} %wv.1, bf16[64,1024]{1,0:T(8,128)(2,1)} %bitcast.8, f32[2,512,128]{2,1,0:T(8,128)} %pad_maximum_fusion.cosine, ...), custom_call_target="tpu_custom_call" | custom-call | tf_op jit(solution)/shard_map/pallas_call | solution.py:598
  171.6 2.3 %copy.11 = bf16[128,4096]{1,0:T(8,128)(2,1)} copy(bf16[128,4096]{1,0:T(8,128)(2,1)} %shard_map.73) | data formatting | bytes 2097152
  (5 shorter events, 0.0 us)
Async XLA Ops:
  0.0 0.7 copy-start

commit v3 on v2

--- a/solution.py
+++ b/solution.py
@@ -2,6 +2,7 @@
 
 import jax
 import jax.numpy as jnp
+import numpy as np
 from jax import lax
 from jax.experimental import pallas as pl
 from jax.experimental.pallas import tpu as pltpu
@@ -22,6 +23,8 @@
 Y_OFFSETS = [0, -1, 1, 2]
 COPIES_A = 8 + 32
 COPIES_B = 4 + 32
+RELAY_COPIES = 17
+PRODUCT_COPIES = 14
 Q_A = 384
 O_A = 384
 NT = (((1,), (1,)), ((), ()))
@@ -182,15 +185,18 @@
         out = [[self.begin]]
         for hop in range(1, ring // 2 + 1):
             out.append([functools.partial(self.first_arrival, hop)])
-        born = [0] + [(b + 1) // 2 for b in range(1, blocks)]
-        pace = 2 if self.z_first else 4
         for b in range(blocks):
-            for hop in range(1, across // 2 + 1):
-                at = max(born[b] + hop, b * across * 3 // 2 // (2 * pace) + hop)
+            for hop in range(1, across // 2):
+                at = (b + 1) // 2 + hop
                 while len(out) <= at:
                     out.append([])
                 out[at].append(functools.partial(self.second_arrival, b, hop))
         return out
+
+    def rest(self):
+        blocks, across = (NZ, NY) if self.z_first else (NY, NZ)
+        for b in range(blocks):
+            self.second_arrival(b, across // 2)
 
 
 class Tokens:
@@ -244,69 +250,75 @@
 class Relay:
     def __init__(self, here, copies, kv, hops):
         self.here, self.copies, self.kv, self.hops = here, copies, kv, hops
-        self.first = copies.reserve(10)
-
-    def slot(self, kind, distance, xl=None):
-        rows = pl.ds((SPAN - 1 - distance) * self.rows(), self.rows())
-        return self.kv.at[kind, :, rows] if xl is None else self.kv.at[kind, xl, rows]
-
-    def rows(self):
-        return self.kv.shape[2] // SPAN
-
-    def along(self, distance):
-        h = self.here
-        src = self.slot(h.core, 0) if distance == 1 else self.hops.at[distance - 2]
+        self.first = copies.reserve(RELAY_COPIES)
+        self.count = kv.shape[2] // SPAN
+
+    def rows(self, distance, offset=0):
+        skipped = BLOCK if distance == SPAN - 1 else 0
+        return pl.ds(offset + skipped, self.count - skipped)
+
+    def slot(self, kind, distance, xl):
+        return self.kv.at[kind, xl, self.rows(distance, (SPAN - 1 - distance) * self.count)]
+
+    def hop(self, distance, xl, needed=None):
+        rows = self.rows(distance if needed is None else needed)
+        return self.hops.at[distance - 1, xl, rows]
+
+    def along(self, distance, xl):
+        h = self.here
+        if distance > 1:
+            src = self.hop(distance - 1, xl, distance)
+        else:
+            src = self.slot(h.core, 0, xl)
         return self.copies.make(
-            self.first + distance - 1,
-            src,
-            self.hops.at[distance - 1],
-            device(h.y, h.x, h.z + 1, h.core),
+            self.first + 2 * (distance - 1) + xl, src, self.hop(distance, xl), device(h.y, h.x, h.z + 1, h.core)
         )
 
     def over(self, distance):
         h = self.here
         return self.copies.make(
-            self.first + 2 + distance,
-            self.hops.at[distance - 1, 1],
+            self.first + 5 + distance,
+            self.hop(distance, 1),
             self.slot(h.core, distance, 0),
             device(h.y + 1, h.x, h.z, h.core),
         )
 
-    def beside(self, distance, sending):
-        h = self.here
-        ref = self.slot(h.core if sending else 1 - h.core, distance)
-        return self.copies.make(self.first + 6 + distance, ref, ref, device(h.y, h.x, h.z, 1 - h.core))
-
-    def begin(self):
-        self.copies.send(self.along(1))
-        self.copies.send(self.beside(0, True))
-
-    def arrival(self, distance):
-        h = self.here
-        self.along(distance).wait_recv()
+    def beside(self, distance, xl, sending):
+        h = self.here
+        ref = self.slot(h.core if sending else 1 - h.core, distance, xl)
+        return self.copies.make(
+            self.first + 9 + 2 * distance + xl, ref, ref, device(h.y, h.x, h.z, 1 - h.core)
+        )
+
+    def begin(self, xl):
+        self.copies.send(self.along(1, xl))
+        self.copies.send(self.beside(0, xl, True))
+
+    def place(self, distance, xl, source):
+        at = self.rows(distance, (SPAN - 1 - distance) * self.count)
+        self.kv[self.here.core, xl, at] = self.hops[distance - 1, source, self.rows(distance)]
+
+    def arrival(self, distance, xl):
+        wrapped = self.here.z < distance
+        self.along(distance, xl).wait_recv()
         if distance < SPAN - 1:
-            self.copies.send(self.along(distance + 1))
-        wrapped = h.z < distance
-        start = (SPAN - 1 - distance) * self.rows()
-        rows = pl.ds(start, self.rows())
-        self.copies.send(self.over(distance), wrapped)
-
-        @pl.when(wrapped)
-        def _():
-            self.kv[h.core, 1, rows] = self.hops[distance - 1, 0]
-
-        @pl.when(jnp.logical_not(wrapped))
-        def _():
-            self.kv[h.core, 0, rows] = self.hops[distance - 1, 0]
-            self.kv[h.core, 1, rows] = self.hops[distance - 1, 1]
+            self.copies.send(self.along(distance + 1, xl))
+        if xl == 1:
+            self.copies.send(self.over(distance), wrapped)
+            pl.when(jnp.logical_not(wrapped))(lambda: self.place(distance, 1, 1))
+        else:
+            pl.when(wrapped)(lambda: self.place(distance, 1, 0))
+            pl.when(jnp.logical_not(wrapped))(lambda: self.place(distance, 0, 0))
+            self.copies.send(self.beside(distance, 1, True))
 
     def placed(self, distance):
         pl.when(self.here.z < distance)(self.over(distance).wait_recv)
-        self.copies.send(self.beside(distance, True))
+        self.copies.send(self.beside(distance, 0, True))
 
     def rest(self):
         for distance in range(SPAN):
-            self.beside(distance, False).wait_recv()
+            for xl in range(NX):
+                self.beside(distance, xl, False).wait_recv()
 
 
 class Products:
@@ -314,18 +326,18 @@
         self.here, self.copies, self.own, self.other = here, copies, own, other
         self.half_way = {1: part_a, -1: part_b}
         self.whole = {1: whole_a, -1: whole_b}
-        self.first = copies.reserve(10)
+        self.first = copies.reserve(PRODUCT_COPIES)
         self.width = own.shape[-1] // 2
 
     def columns(self, half):
         return pl.ds(half * self.width, self.width)
 
-    def beside(self, j):
+    def beside(self, j, half):
         h = self.here
         return self.copies.make(
-            self.first + j,
-            self.own.at[1 - h.core, j],
-            self.other.at[j],
+            self.first + 6 + 2 * j + half,
+            self.own.at[1 - h.core, j, :, self.columns(half)],
+            self.other.at[j, :, self.columns(half)],
             device(h.y, h.x, h.z, 1 - h.core),
         )
 
@@ -333,7 +345,7 @@
         h = self.here
         half = 0 if direction > 0 else 1
         return self.copies.make(
-            self.first + 4 + half,
+            self.first + half,
             self.own.at[h.core, 0, :, self.columns(half)],
             self.half_way[direction],
             device(h.y, h.x + direction, h.z, h.core),
@@ -343,7 +355,7 @@
         h = self.here
         j = 1 if direction > 0 else 2
         return self.copies.make(
-            self.first + 6 + 2 * (j - 1) + half,
+            self.first + 2 * j + half,
             self.own.at[h.core, j, :, self.columns(half)],
             self.whole[direction].at[:, self.columns(half)],
             device(h.y, h.x + direction, h.z, h.core),
@@ -365,16 +377,15 @@
         lax.fori_loop(0, self.width // tile, body, 0)
 
     def reduce(self, j):
-        self.beside(j).wait_recv()
-        if j == 0:
-            for direction in (1, -1):
-                self.add(0, 0 if direction > 0 else 1)
-                self.copies.send(self.far(direction))
-        elif j < 3:
-            direction = 1 if j == 1 else -1
-            half = 1 if direction > 0 else 0
-            self.add(j, half)
-            self.copies.send(self.near(direction, half))
+        order = (1, 0) if j == 1 else (0, 1)
+        for turn, half in enumerate(order):
+            self.beside(j, half).wait_recv()
+            if j == 0:
+                self.add(0, half)
+                self.copies.send(self.far(1 if half == 0 else -1))
+            elif j < 3 and turn == 0:
+                self.add(j, half)
+                self.copies.send(self.near(1 if j == 1 else -1, half))
 
     def last(self, out):
         h = self.here
@@ -414,9 +425,9 @@
 
 
 def block_kernel(
-    tokens, gain, wq, wk, wv, wo, cosine, sine, bias, out,
+    docs, tokens, gain, wq, wk, wv, wo, inner_cos, inner_sin, outer_cos, outer_sin, out,
     rows, qa, qb, qb_own, oa, ob, queries, kv, values, hops, attended,
-    own, other, part_a, part_b, whole_a, whole_b, send_sems, recv_sems,
+    own, other, part_a, part_b, whole_a, whole_b, cosine, sine, bias, send_sems, recv_sems,
 ):
     h = Place()
     half_heads = wq.shape[1] // 2
@@ -429,6 +440,16 @@
         qb_own[p, :, :HD] = wq[:, p * half_heads + Q_A : (p + 1) * half_heads]
         qb_own[p, :, HD:] = kind[...]
 
+    copies = Copies(send_sems, recv_sems)
+    gathers = [Gather(h, copies, buf, z_first) for buf, z_first in ((qa, True), (qb, False), (oa, True), (ob, False))]
+    token_rows = Tokens(h, copies, rows)
+    relay = Relay(h, copies, kv, hops)
+    products = Products(h, copies, own, other, part_a, part_b, whole_a, whole_b)
+
+    pl.semaphore_wait(barrier, len(greeted))
+    gathers[0].exchange([wq.at[:, pl.ds(p * half_heads, Q_A)] for p in (0, 1)])
+    gathers[1].exchange([qb_own.at[p] for p in (0, 1)])
+
     def norm(step, _):
         at = pl.ds(pl.multiple_of(step * 32, 32), 32)
         value = tokens[at, :].astype(jnp.float32)
@@ -437,38 +458,55 @@
         return 0
 
     lax.fori_loop(0, BLOCK // 32, norm, 0)
-    pl.semaphore_wait(barrier, len(greeted))
-
-    copies = Copies(send_sems, recv_sems)
-    gathers = [Gather(h, copies, buf, z_first) for buf, z_first in ((qa, True), (qb, False), (oa, True), (ob, False))]
-    token_rows = Tokens(h, copies, rows)
-    relay = Relay(h, copies, kv, hops)
-    products = Products(h, copies, own, other, part_a, part_b, whole_a, whole_b)
-
-    gathers[0].exchange([wq.at[:, pl.ds(p * half_heads, Q_A)] for p in (0, 1)])
-    gathers[1].exchange([qb_own.at[p] for p in (0, 1)])
     token_rows.begin()
-    gathers[2].exchange([wo.at[:, pl.ds(p * half_heads, O_A)] for p in (0, 1)])
-    gathers[3].exchange([wo.at[:, pl.ds(p * half_heads + O_A, half_heads - O_A)] for p in (0, 1)])
 
     plans = [part.stages() for part in gathers]
+    lengths = [len(plan) for plan in plans]
 
     def run(which, stage):
         for index in which:
-            if 0 <= stage < len(plans[index]):
+            if 0 <= stage < lengths[index]:
                 for step in plans[index][stage]:
                     step()
 
-    first_stages = max(len(plans[0]), len(plans[1]))
-    last_stages = max(len(plans[2]), len(plans[3]))
-    early = 3
-    for stage in range(first_stages):
+    def fill_tables():
+        for xl in range(NX):
+            context = (h.y * NX + xl) * NZ + h.z
+            oc, os_ = outer_cos[context], outer_sin[context]
+            cosine[xl] = inner_cos[...] * oc - inner_sin[...] * os_
+            turned = inner_sin[...] * oc + inner_cos[...] * os_
+            lane = lax.broadcasted_iota(jnp.int32, turned.shape, 1)
+            sine[xl] = jnp.where(lane < HD // 2, -turned, turned)
+
+        def mask(index, _):
+            block = ((h.y * NX + index // NTP) * NZ + h.z) * NTP + lax.rem(index, NTP)
+            for w in range(WINDOW):
+                key = block - (WINDOW - 1) + w
+                same = docs[lax.rem(key + docs.shape[0], docs.shape[0])] == docs[block]
+                visible = jnp.logical_and(same, key >= 0)
+                bias[index, :, w * BLOCK : (w + 1) * BLOCK] = jnp.full(
+                    (1, BLOCK), jnp.where(visible, 0.0, neg_large), jnp.float32
+                )
+            return 0
+
+        lax.fori_loop(0, NX * NTP, mask, 0)
+        values[:, :, HD:] = jnp.ones_like(values[:, :, HD:])
+
+    lag = 3
+    for stage in range(max(lengths[:2])):
         run((0, 1), stage)
-        run((2, 3), stage - (first_stages - early))
-        if stage == 4:
+        if stage == 0:
+            gathers[2].exchange([wo.at[:, pl.ds(p * half_heads, O_A)] for p in (0, 1)])
+            gathers[3].exchange([wo.at[:, pl.ds(p * half_heads + O_A, half_heads - O_A)] for p in (0, 1)])
+            fill_tables()
+        if stage == 2:
             token_rows.first_hop(0)
-        if stage == first_stages - 2:
+        if stage == 5:
             token_rows.first_hop(1)
+        run((2, 3), stage - lag)
+    stage = max(lengths[:2]) - lag
+    gathers[0].rest()
+    gathers[1].rest()
     token_rows.second_hop()
     token_rows.rest()
 
@@ -509,21 +547,28 @@
             keep_query(total[:, head * HD : (head + 1) * HD], chip, head)
         return 0
 
-    lax.fori_loop(0, RING_X, project_b, 0)
-    relay.begin()
-    run((2, 3), early)
-    lax.fori_loop(0, RING_X, project_a, 0)
-    stage = early + 1
+    for xl in (1, 0):
+        lax.fori_loop(0, RING_X // NX, lambda xh, _: project_b(xh * 2 + xl, 0), 0)
+        relay.begin(xl)
+    run((2, 3), stage)
+    lax.fori_loop(0, RING_X // 2, project_a, 0)
+    run((2, 3), stage + 1)
+    lax.fori_loop(RING_X // 2, RING_X, project_a, 0)
+    stage += 2
     for distance in range(1, SPAN):
-        relay.arrival(distance)
+        for xl in (1, 0):
+            relay.arrival(distance, xl)
+        if distance > 1:
+            relay.placed(distance - 1)
         run((2, 3), stage)
         stage += 1
-        relay.placed(distance)
-    for stage in range(stage, last_stages):
+    relay.placed(SPAN - 1)
+    for stage in range(stage, max(lengths[2:])):
         run((2, 3), stage)
     relay.rest()
-
-    values[:, :, HD:] = jnp.ones_like(values[:, :, HD:])
+    gathers[2].rest()
+    gathers[3].rest()
+
     for xl in range(NX):
         values[xl, :, :HD] = kv[1, xl]
 
@@ -555,7 +600,7 @@
 
         lax.fori_loop(0, 2, body, 0)
 
-    def multiply(j, chip):
+    def multiply(j, chip, half):
         xl, first_block = lax.rem(chip, 2), (chip // 2) * 2
         tile = NZ * wo.shape[0]
 
@@ -571,34 +616,47 @@
                 own[core, j, :, at] = total[core * BLOCK : (core + 1) * BLOCK]
             return 0
 
-        lax.fori_loop(0, NY * NX, body, 0)
+        lax.fori_loop(half * (NY * NX // 2), (half + 1) * (NY * NX // 2), body, 0)
 
     for j, offset in enumerate((2, 1, 3, 0)):
         chip = lax.rem(h.x + offset, RING_X)
         attend(chip)
-        if j > 0:
+        if j > 1:
             products.reduce(j - 1)
-        multiply(j, chip)
-        copies.send(products.beside(j))
+        for half in (0, 1):
+            multiply(j, chip, half)
+            copies.send(products.beside(j, half))
+        if j == 0:
+            products.reduce(0)
     products.reduce(3)
     products.last(out)
     copies.finish()
 
 
-COPIES = 2 * (COPIES_A + COPIES_B + 4) + 13 + 10 + 10
-
-
-def whole_block(tokens, gain, w_query, w_key, w_value, w_out_t, cosine, sine, bias):
+COPIES = 2 * (COPIES_A + COPIES_B + 4) + 13 + RELAY_COPIES + PRODUCT_COPIES
+
+
+def rotation_tables(count):
+    half_width = HD // 2
+    frequency = np.float32(rope_base) ** (-np.arange(half_width, dtype=np.float32) / np.float32(half_width))
+    frequency = np.concatenate([frequency, frequency]).astype(np.float64)
+    inner = np.arange(count)[:, None] * frequency
+    outer = (np.arange(NY * NX * NZ) * count)[:, None, None] * frequency
+    return [f(angle).astype(np.float32) for angle in (inner, outer) for f in (np.cos, np.sin)]
+
+
+def whole_block(doc_blocks, tokens, gain, w_query, w_key, w_value, w_out_t):
     count, width = tokens.shape
     rows = w_query.shape[0]
     half = w_query.shape[1] // 2
     near = NTP * count
     bf16 = jnp.bfloat16
     vmem = pl.BlockSpec(memory_space=pltpu.VMEM)
+    turns = rotation_tables(near)
     return pl.pallas_call(
         block_kernel,
         out_shape=jax.ShapeDtypeStruct((count, width), bf16),
-        in_specs=[vmem] * 9,
+        in_specs=[pl.BlockSpec(memory_space=pltpu.SMEM)] + [vmem] * 10,
         out_specs=vmem,
         scratch_shapes=[
             pltpu.VMEM((NX, NTP, count, width), bf16),
@@ -618,37 +676,20 @@
             pltpu.VMEM((count, width // 2), bf16),
             pltpu.VMEM((count, width), bf16),
             pltpu.VMEM((count, width), bf16),
+            pltpu.VMEM((NX, near, HD), jnp.float32),
+            pltpu.VMEM((NX, near, HD), jnp.float32),
+            pltpu.VMEM((NX * NTP, 1, WINDOW * BLOCK), jnp.float32),
             pltpu.SemaphoreType.DMA((COPIES,)),
             pltpu.SemaphoreType.DMA((COPIES,)),
         ],
         compiler_params=pltpu.CompilerParams(
             collective_id=0, has_side_effects=True, vmem_limit_bytes=60 * 1024 * 1024
         ),
-    )(tokens, gain, w_query, w_key, w_value, w_out_t, cosine, sine, bias)
-
-
-def tables(doc_blocks, count):
-    c = lax.axis_index("ctx")
-    y, z = c // (NX * NZ), lax.rem(c, NZ)
-    contexts = y * (NX * NZ) + jnp.arange(NX, dtype=jnp.int32) * NZ + z
-    positions = contexts[:, None] * (NTP * count) + jnp.arange(NTP * count, dtype=jnp.int32)[None, :]
-    half_width = HD // 2
-    frequency = rope_base ** (-jnp.arange(half_width, dtype=jnp.float32) / half_width)
-    angles = positions.astype(jnp.float32)[..., None] * frequency
-    cosine, sine = jnp.cos(angles), jnp.sin(angles)
-    cosine = jnp.concatenate([cosine, cosine], axis=-1)
-    sine = jnp.concatenate([-sine, sine], axis=-1)
-    blocks = (contexts[:, None] * NTP + jnp.arange(NTP, dtype=jnp.int32)).reshape(-1)
-    keys = blocks[:, None] - (WINDOW - 1) + jnp.arange(WINDOW, dtype=jnp.int32)
-    visible = (keys >= 0) & (doc_blocks[jnp.maximum(keys, 0)] == doc_blocks[blocks][:, None])
-    bias = jnp.where(visible, 0.0, neg_large).astype(jnp.float32)
-    bias = jnp.broadcast_to(bias[:, None, :, None], (NX * NTP, 1, WINDOW, BLOCK)).reshape(NX * NTP, 1, WINDOW * BLOCK)
-    return cosine, sine, bias
+    )(doc_blocks, tokens, gain, w_query, w_key, w_value, w_out_t, *turns)
 
 
 def local(tokens, norm_gain, w_query, w_key, w_value, w_out, doc_blocks):
-    cosine, sine, bias = tables(doc_blocks, tokens.shape[0])
-    return whole_block(tokens, norm_gain[None, :], w_query, w_key, w_value, w_out.T, cosine, sine, bias)
+    return whole_block(doc_blocks, tokens, norm_gain[None, :], w_query, w_key, w_value, w_out.T)
 
 
 def solution(mesh):

time: 174 us -> 144 us (0.83); the launches traced: 174 us -> 142 us
  Pallas kernels: 164 us -> 140 us
  other arithmetic: 4.24 us -> 0 us
  local copies, waits for them, and re-layouts: 5.77 us -> 2.29 us
    pallas_call x1, Pallas kernels: 164 us -> 140 us  [whole_block(): pl.pallas_call(block_kernel, out_shape=jax.ShapeDtypeStruct((count, width...]
    concatenate x2 -> x0, other arithmetic: 2.01 us -> none  [the longest x1 1.02 us: tables(): sine = jnp.concatenate([-sine, sine], axis=-1)]
    gather x3 -> x0, local copies, waits for them, and re-layouts: 1.99 us -> none  [the longest x2 1.35 us: tables(): doc_blocks[jnp.maximum(keys, 0)] == doc_blocks[blocks][:, None]]
    neg x1 -> x0, other arithmetic: 1.9 us -> none  [tables(): sine = jnp.concatenate([-sine, sine], axis=-1)]
where the time goes in v3:
time: 144 us; the launch traced here: 142 us
  Pallas kernels  140 us (97%)
  local copies, waits for them, and re-layouts  2.29 us (2%)
    pallas_call x1, Pallas kernels, whole_block(): pl.pallas_call(block_kernel, out_shape=jax.ShapeDtypeStruct((count, width...  140 us

profile of v3, /device:TPU:38, one launch (start us, length us, event | category | flops | bytes accessed | tf_op | source)
XLA Modules:
  0.0 142.1 jit_solution(18015868772557584317)
XLA Ops:
  0.0 139.8 %shard_map.109 = bf16[128,4096]{1,0:T(8,128)(2,1)} custom-call(s32[256]{0:T(256)} %docs.1, bf16[128,4096]{1,0:T(8,128)(2,1)} %tokens.1, f32[1,4096]{1,0:T(1,128)} %bitcast.3, bf16[64,1024]{1,0:T(8,128)(2,1)} %wq.1, bf16[64,128]{1,0:T(8,128)(2,1)} %wk.1, bf16[64,128]{1,0:T(8,128)(2,1)} %wv.1, bf16[64,1024]{1,0:T(8,128)(2,1)} %bitcast.2, ...), custom_call_target="tpu_custom_call" | custom-call | tf_op jit(solution)/shard_map/pallas_call | solution.py:656
  139.9 2.3 %copy.13 = bf16[128,4096]{1,0:T(8,128)(2,1)} copy(bf16[128,4096]{1,0:T(8,128)(2,1)} %shard_map.109) | data formatting | bytes 2097152

commit v4 on v3

--- a/solution.py
+++ b/solution.py
@@ -21,12 +21,12 @@
 
 Z_OFFSETS = [0, -1, 1, -2, 2, -3, 3, 4]
 Y_OFFSETS = [0, -1, 1, 2]
+TILE_OFFSETS = [0, 1, -1, 2]
 COPIES_A = 8 + 32
 COPIES_B = 4 + 32
 RELAY_COPIES = 17
-PRODUCT_COPIES = 14
+PRODUCT_COPIES = 14 * NY
 Q_A = 384
-O_A = 384
 NT = (((1,), (1,)), ((), ()))
 
 
@@ -199,6 +199,46 @@
             self.second_arrival(b, across // 2)
 
 
+class Columns(Gather):
+    def __init__(self, here, copies, buf):
+        super().__init__(here, copies, buf, True)
+
+    def across(self, block, direction, hop, sending):
+        h = self.here
+        return self.copy(
+            self.ring_id(True, block, direction, hop, NY),
+            h.y - direction * (hop - 1 if sending else hop),
+            h.z + Z_OFFSETS[block],
+            None,
+            device(h.y + direction, h.x, h.z, h.core),
+        )
+
+    def ring_begin(self):
+        self.exchanged()
+        for direction in (1, -1):
+            self.copies.send(self.first_ring(direction, 1, True))
+
+    def ring_arrival(self, hop):
+        for direction in (1, -1):
+            self.first_ring(direction, hop, False).wait_recv()
+            if hop < NZ // 2:
+                self.copies.send(self.first_ring(direction, hop + 1, True))
+
+    def send_across(self, direction, blocks=range(NZ)):
+        for block in blocks:
+            self.copies.send(self.across(block, direction, 1, True))
+
+    def pass_across(self, blocks):
+        for block in blocks:
+            self.across(block, -1, 1, False).wait_recv()
+            self.copies.send(self.across(block, -1, 2, True))
+
+    def await_tile(self, tile):
+        if tile >= 2:
+            for block in range(NZ):
+                self.across(block, 1 if tile == 2 else -1, tile - 1 if tile == 2 else 2, False).wait_recv()
+
+
 class Tokens:
     def __init__(self, here, copies, rows):
         self.here, self.copies, self.rows = here, copies, rows
@@ -327,87 +367,81 @@
         self.half_way = {1: part_a, -1: part_b}
         self.whole = {1: whole_a, -1: whole_b}
         self.first = copies.reserve(PRODUCT_COPIES)
-        self.width = own.shape[-1] // 2
-
-    def columns(self, half):
-        return pl.ds(half * self.width, self.width)
-
-    def beside(self, j, half):
+        self.width = own.shape[-1]
+
+    def columns(self, tile, half):
+        y = lax.rem(self.here.y + TILE_OFFSETS[tile] + NY, NY)
+        return pl.ds(pl.multiple_of((2 * y + half) * self.width, self.width), self.width)
+
+    def beside(self, tile, j, half):
         h = self.here
         return self.copies.make(
-            self.first + 6 + 2 * j + half,
-            self.own.at[1 - h.core, j, :, self.columns(half)],
-            self.other.at[j, :, self.columns(half)],
+            self.first + 14 * tile + 6 + 2 * j + half,
+            self.own.at[1 - h.core, j, 2 * tile + half],
+            self.other.at[j, 2 * tile + half],
             device(h.y, h.x, h.z, 1 - h.core),
         )
 
-    def far(self, direction):
+    def far_place(self, tile, direction):
+        return self.half_way[direction].at[tile]
+
+    def far(self, tile, direction):
         h = self.here
         half = 0 if direction > 0 else 1
         return self.copies.make(
-            self.first + half,
-            self.own.at[h.core, 0, :, self.columns(half)],
-            self.half_way[direction],
+            self.first + 14 * tile + half,
+            self.own.at[h.core, 0, 2 * tile + half],
+            self.far_place(tile, direction),
             device(h.y, h.x + direction, h.z, h.core),
         )
 
-    def near(self, direction, half):
+    def near(self, tile, direction, half):
         h = self.here
         j = 1 if direction > 0 else 2
         return self.copies.make(
-            self.first + 2 * j + half,
-            self.own.at[h.core, j, :, self.columns(half)],
-            self.whole[direction].at[:, self.columns(half)],
+            self.first + 14 * tile + 2 * j + half,
+            self.own.at[h.core, j, 2 * tile + half],
+            self.whole[direction].at[2 * tile + half],
             device(h.y, h.x + direction, h.z, h.core),
         )
 
-    def add(self, j, half, more=None):
-        h = self.here
-        tile = 512
-
-        def body(step, _):
-            inner = pl.multiple_of(step * tile, tile)
-            at = pl.ds(pl.multiple_of(half * self.width + inner, tile), tile)
-            total = self.own[h.core, j, :, at].astype(jnp.float32) + self.other[j, :, at].astype(jnp.float32)
-            if more is not None:
-                total = total + more[:, pl.ds(inner, tile)].astype(jnp.float32)
-            self.own[h.core, j, :, at] = total.astype(jnp.bfloat16)
-            return 0
-
-        lax.fori_loop(0, self.width // tile, body, 0)
-
-    def reduce(self, j):
+    def add(self, tile, j, half, more=None):
+        h = self.here
+        at = 2 * tile + half
+        total = self.own[h.core, j, at].astype(jnp.float32) + self.other[j, at].astype(jnp.float32)
+        if more is not None:
+            total = total + more[...].astype(jnp.float32)
+        self.own[h.core, j, at] = total.astype(jnp.bfloat16)
+
+    def reduce(self, tile, j):
         order = (1, 0) if j == 1 else (0, 1)
         for turn, half in enumerate(order):
-            self.beside(j, half).wait_recv()
+            self.beside(tile, j, half).wait_recv()
             if j == 0:
-                self.add(0, half)
-                self.copies.send(self.far(1 if half == 0 else -1))
+                self.add(tile, 0, half)
+                self.copies.send(self.far(tile, 1 if half == 0 else -1))
             elif j < 3 and turn == 0:
-                self.add(j, half)
-                self.copies.send(self.near(1 if j == 1 else -1, half))
-
-    def last(self, out):
-        h = self.here
+                self.add(tile, j, half)
+                self.copies.send(self.near(tile, 1 if j == 1 else -1, half))
+
+    def pass_on(self, tile):
         for direction in (1, -1):
             j, half = (1, 0) if direction > 0 else (2, 1)
-            self.far(direction).wait_recv()
-            self.add(j, half, self.half_way[direction])
-            self.copies.send(self.near(direction, half))
+            self.far(tile, direction).wait_recv()
+            self.add(tile, j, half, self.far_place(tile, direction))
+            self.copies.send(self.near(tile, direction, half))
+
+    def last(self, tile, out):
+        h = self.here
         for half in (0, 1):
             for direction in (1, -1):
-                self.near(direction, half).wait_recv()
-        tile = 512
-
-        def body(step, _):
-            at = pl.ds(pl.multiple_of(step * tile, tile), tile)
-            total = self.own[h.core, 3, :, at].astype(jnp.float32) + self.other[3, :, at].astype(jnp.float32)
+                self.near(tile, direction, half).wait_recv()
+        for half in (0, 1):
+            at = 2 * tile + half
+            total = self.own[h.core, 3, at].astype(jnp.float32) + self.other[3, at].astype(jnp.float32)
             for direction in (1, -1):
-                total = total + self.whole[direction][:, at].astype(jnp.float32)
-            out[:, at] = total.astype(out.dtype)
-            return 0
-
-        lax.fori_loop(0, 2 * self.width // tile, body, 0)
+                total = total + self.whole[direction][at].astype(jnp.float32)
+            out[:, self.columns(tile, half)] = total.astype(out.dtype)
 
 
 def neighbours(h):
@@ -426,7 +460,7 @@
 
 def block_kernel(
     docs, tokens, gain, wq, wk, wv, wo, inner_cos, inner_sin, outer_cos, outer_sin, out,
-    rows, qa, qb, qb_own, oa, ob, queries, kv, values, hops, attended,
+    rows, qa, qb, qb_own, oa, queries, kv, values, hops, attended,
     own, other, part_a, part_b, whole_a, whole_b, cosine, sine, bias, send_sems, recv_sems,
 ):
     h = Place()
@@ -441,7 +475,8 @@
         qb_own[p, :, HD:] = kind[...]
 
     copies = Copies(send_sems, recv_sems)
-    gathers = [Gather(h, copies, buf, z_first) for buf, z_first in ((qa, True), (qb, False), (oa, True), (ob, False))]
+    gathers = [Gather(h, copies, buf, z_first) for buf, z_first in ((qa, True), (qb, False))]
+    columns = Columns(h, copies, oa)
     token_rows = Tokens(h, copies, rows)
     relay = Relay(h, copies, kv, hops)
     products = Products(h, copies, own, other, part_a, part_b, whole_a, whole_b)
@@ -449,6 +484,7 @@
     pl.semaphore_wait(barrier, len(greeted))
     gathers[0].exchange([wq.at[:, pl.ds(p * half_heads, Q_A)] for p in (0, 1)])
     gathers[1].exchange([qb_own.at[p] for p in (0, 1)])
+    columns.exchange([wo.at[:, pl.ds(p * half_heads, half_heads)] for p in (0, 1)])
 
     def norm(step, _):
         at = pl.ds(pl.multiple_of(step * 32, 32), 32)
@@ -461,12 +497,11 @@
     token_rows.begin()
 
     plans = [part.stages() for part in gathers]
-    lengths = [len(plan) for plan in plans]
-
-    def run(which, stage):
-        for index in which:
-            if 0 <= stage < lengths[index]:
-                for step in plans[index][stage]:
+
+    def run(stage):
+        for plan in plans:
+            if stage < len(plan):
+                for step in plan[stage]:
                     step()
 
     def fill_tables():
@@ -492,21 +527,23 @@
         lax.fori_loop(0, NX * NTP, mask, 0)
         values[:, :, HD:] = jnp.ones_like(values[:, :, HD:])
 
-    lag = 3
-    for stage in range(max(lengths[:2])):
-        run((0, 1), stage)
+    for stage in range(max(len(plan) for plan in plans)):
+        run(stage)
         if stage == 0:
-            gathers[2].exchange([wo.at[:, pl.ds(p * half_heads, O_A)] for p in (0, 1)])
-            gathers[3].exchange([wo.at[:, pl.ds(p * half_heads + O_A, half_heads - O_A)] for p in (0, 1)])
             fill_tables()
         if stage == 2:
             token_rows.first_hop(0)
+            columns.ring_begin()
+        if stage == 4:
+            columns.ring_arrival(1)
         if stage == 5:
             token_rows.first_hop(1)
-        run((2, 3), stage - lag)
-    stage = max(lengths[:2]) - lag
+            columns.ring_arrival(2)
     gathers[0].rest()
     gathers[1].rest()
+    columns.send_across(-1, range(5))
+    columns.ring_arrival(3)
+    columns.send_across(-1, range(5, 7))
     token_rows.second_hop()
     token_rows.rest()
 
@@ -550,24 +587,18 @@
     for xl in (1, 0):
         lax.fori_loop(0, RING_X // NX, lambda xh, _: project_b(xh * 2 + xl, 0), 0)
         relay.begin(xl)
-    run((2, 3), stage)
-    lax.fori_loop(0, RING_X // 2, project_a, 0)
-    run((2, 3), stage + 1)
-    lax.fori_loop(RING_X // 2, RING_X, project_a, 0)
-    stage += 2
+    lax.fori_loop(0, RING_X, project_a, 0)
+    columns.ring_arrival(4)
+    columns.send_across(-1, range(7, NZ))
     for distance in range(1, SPAN):
         for xl in (1, 0):
             relay.arrival(distance, xl)
         if distance > 1:
             relay.placed(distance - 1)
-        run((2, 3), stage)
-        stage += 1
+        columns.pass_across(range(2 * distance - 2, 2 * distance))
     relay.placed(SPAN - 1)
-    for stage in range(stage, max(lengths[2:])):
-        run((2, 3), stage)
+    columns.send_across(1)
     relay.rest()
-    gathers[2].rest()
-    gathers[3].rest()
 
     for xl in range(NX):
         values[xl, :, :HD] = kv[1, xl]
@@ -600,40 +631,48 @@
 
         lax.fori_loop(0, 2, body, 0)
 
-    def multiply(j, chip, half):
-        xl, first_block = lax.rem(chip, 2), (chip // 2) * 2
-        tile = NZ * wo.shape[0]
-
-        def body(step, _):
-            left = attended[xl, pl.ds(first_block, 2)].reshape(2 * BLOCK, half_heads)
-            y, x = step // NX, lax.rem(step, NX)
-            right = jnp.concatenate(
-                [oa[y, x].reshape(tile, O_A), ob[y, x].reshape(tile, half_heads - O_A)], axis=1
-            )
+    order = (2, 1, 3, 0)
+
+    def multiply(tile, j):
+        chip = lax.rem(h.x + order[j], RING_X)
+        left = attended[lax.rem(chip, 2), pl.ds((chip // 2) * 2, 2)].reshape(2 * BLOCK, half_heads)
+        y = lax.rem(h.y + TILE_OFFSETS[tile] + NY, NY)
+        depth = NZ * wo.shape[0]
+
+        for half in (0, 1):
+            right = oa[y, half].reshape(depth, half_heads)
             total = lax.dot_general(left, right, NT, preferred_element_type=jnp.float32).astype(jnp.bfloat16)
-            at = pl.ds(pl.multiple_of(step * tile, tile), tile)
             for core in (0, 1):
-                own[core, j, :, at] = total[core * BLOCK : (core + 1) * BLOCK]
-            return 0
-
-        lax.fori_loop(half * (NY * NX // 2), (half + 1) * (NY * NX // 2), body, 0)
-
-    for j, offset in enumerate((2, 1, 3, 0)):
-        chip = lax.rem(h.x + offset, RING_X)
-        attend(chip)
+                own[core, j, 2 * tile + half] = total[core * BLOCK : (core + 1) * BLOCK]
+            copies.send(products.beside(tile, j, half))
+
+    for j in range(RING_X):
+        attend(lax.rem(h.x + order[j], RING_X))
         if j > 1:
-            products.reduce(j - 1)
-        for half in (0, 1):
-            multiply(j, chip, half)
-            copies.send(products.beside(j, half))
+            products.reduce(0, j - 1)
+        multiply(0, j)
         if j == 0:
-            products.reduce(0)
-    products.reduce(3)
-    products.last(out)
+            products.reduce(0, 0)
+    products.pass_on(0)
+    columns.pass_across(range(6, NZ))
+    for tile in range(1, NY):
+        columns.await_tile(tile)
+        for j in range(RING_X):
+            multiply(tile, j)
+        products.reduce(tile - 1, 3)
+        products.reduce(tile, 0)
+        if tile > 1:
+            products.pass_on(tile - 1)
+        products.reduce(tile, 1)
+        products.reduce(tile, 2)
+    products.pass_on(NY - 1)
+    products.reduce(NY - 1, 3)
+    for tile in range(NY):
+        products.last(tile, out)
     copies.finish()
 
 
-COPIES = 2 * (COPIES_A + COPIES_B + 4) + 13 + RELAY_COPIES + PRODUCT_COPIES
+COPIES = 2 * COPIES_A + COPIES_B + 6 + 13 + RELAY_COPIES + PRODUCT_COPIES
 
 
 def rotation_tables(count):
@@ -663,19 +702,18 @@
             pltpu.VMEM((NY, NX, NZ, rows, Q_A), bf16),
             pltpu.VMEM((NY, NX, NZ, rows, half - Q_A + HD), bf16),
             pltpu.VMEM((2, rows, half - Q_A + HD), bf16),
-            pltpu.VMEM((NY, NX, NZ, rows, O_A), bf16),
-            pltpu.VMEM((NY, NX, NZ, rows, half - O_A), bf16),
+            pltpu.VMEM((NY, NX, NZ, rows, half), bf16),
             pltpu.VMEM((NX, NTP, half // HD * BLOCK, HD), bf16),
             pltpu.VMEM((2, NX, SPAN * near, HD), bf16),
             pltpu.VMEM((NX, SPAN * near, 2 * HD), bf16),
             pltpu.VMEM((SPAN - 1, NX, near, HD), bf16),
             pltpu.VMEM((NX, NTP, count, half), bf16),
-            pltpu.VMEM((2, RING_X, count, width), bf16),
-            pltpu.VMEM((RING_X, count, width), bf16),
-            pltpu.VMEM((count, width // 2), bf16),
-            pltpu.VMEM((count, width // 2), bf16),
-            pltpu.VMEM((count, width), bf16),
-            pltpu.VMEM((count, width), bf16),
+            pltpu.VMEM((2, RING_X, 2 * NY, count, width // (2 * NY)), bf16),
+            pltpu.VMEM((RING_X, 2 * NY, count, width // (2 * NY)), bf16),
+            pltpu.VMEM((NY, count, width // (2 * NY)), bf16),
+            pltpu.VMEM((NY, count, width // (2 * NY)), bf16),
+            pltpu.VMEM((2 * NY, count, width // (2 * NY)), bf16),
+            pltpu.VMEM((2 * NY, count, width // (2 * NY)), bf16),
             pltpu.VMEM((NX, near, HD), jnp.float32),
             pltpu.VMEM((NX, near, HD), jnp.float32),
             pltpu.VMEM((NX * NTP, 1, WINDOW * BLOCK), jnp.float32),

time: 144 us -> 136 us (0.944)
  Pallas kernels: 140 us -> 132 us
    pallas_call x1, Pallas kernels: 140 us -> 132 us  [whole_block(): pl.pallas_call(block_kernel, out_shape=jax.ShapeDtypeStruct((count, width...]
where the time goes in v4:
time: 136 us; the launch traced here: 134 us
  Pallas kernels  132 us (97%)
  local copies, waits for them, and re-layouts  2.29 us (2%)
    pallas_call x1, Pallas kernels, whole_block(): pl.pallas_call(block_kernel, out_shape=jax.ShapeDtypeStruct((count, width...  132 us

profile of v4, /device:TPU:38, one launch (start us, length us, event | category | flops | bytes accessed | tf_op | source)
XLA Modules:
  0.0 134.0 jit_solution(3050715911756308762)
XLA Ops:
  0.0 131.7 %shard_map.109 = bf16[128,4096]{1,0:T(8,128)(2,1)} custom-call(s32[256]{0:T(256)} %docs.1, bf16[128,4096]{1,0:T(8,128)(2,1)} %tokens.1, f32[1,4096]{1,0:T(1,128)} %bitcast.3, bf16[64,1024]{1,0:T(8,128)(2,1)} %wq.1, bf16[64,128]{1,0:T(8,128)(2,1)} %wk.1, bf16[64,128]{1,0:T(8,128)(2,1)} %wv.1, bf16[64,1024]{1,0:T(8,128)(2,1)} %bitcast.2, ...), custom_call_target="tpu_custom_call" | custom-call | tf_op jit(solution)/shard_map/pallas_call | solution.py:695
  131.7 2.3 %copy.13 = bf16[128,4096]{1,0:T(8,128)(2,1)} copy(bf16[128,4096]{1,0:T(8,128)(2,1)} %shard_map.109) | data formatting | bytes 2097152

commit v5 on v4

--- a/solution.py
+++ b/solution.py
@@ -481,11 +481,6 @@
     relay = Relay(h, copies, kv, hops)
     products = Products(h, copies, own, other, part_a, part_b, whole_a, whole_b)
 
-    pl.semaphore_wait(barrier, len(greeted))
-    gathers[0].exchange([wq.at[:, pl.ds(p * half_heads, Q_A)] for p in (0, 1)])
-    gathers[1].exchange([qb_own.at[p] for p in (0, 1)])
-    columns.exchange([wo.at[:, pl.ds(p * half_heads, half_heads)] for p in (0, 1)])
-
     def norm(step, _):
         at = pl.ds(pl.multiple_of(step * 32, 32), 32)
         value = tokens[at, :].astype(jnp.float32)
@@ -494,6 +489,11 @@
         return 0
 
     lax.fori_loop(0, BLOCK // 32, norm, 0)
+    pl.semaphore_wait(barrier, len(greeted))
+    gathers[0].exchange([wq.at[:, pl.ds(p * half_heads, Q_A)] for p in (0, 1)])
+    gathers[1].exchange([qb_own.at[p] for p in (0, 1)])
+    columns.exchange([wo.at[:, pl.ds(p * half_heads, half_heads)] for p in (0, 1)])
+
     token_rows.begin()
 
     plans = [part.stages() for part in gathers]
@@ -531,19 +531,17 @@
         run(stage)
         if stage == 0:
             fill_tables()
+        if stage == 1:
+            columns.ring_begin()
         if stage == 2:
             token_rows.first_hop(0)
-            columns.ring_begin()
-        if stage == 4:
-            columns.ring_arrival(1)
+        if stage >= 3:
+            columns.ring_arrival(stage - 2)
         if stage == 5:
             token_rows.first_hop(1)
-            columns.ring_arrival(2)
     gathers[0].rest()
     gathers[1].rest()
-    columns.send_across(-1, range(5))
-    columns.ring_arrival(3)
-    columns.send_across(-1, range(5, 7))
+    columns.send_across(-1, range(7))
     token_rows.second_hop()
     token_rows.rest()
 
@@ -646,27 +644,33 @@
                 own[core, j, 2 * tile + half] = total[core * BLOCK : (core + 1) * BLOCK]
             copies.send(products.beside(tile, j, half))
 
+    columns.pass_across(range(6, NZ))
+    early = (0, 1)
     for j in range(RING_X):
         attend(lax.rem(h.x + order[j], RING_X))
-        if j > 1:
-            products.reduce(0, j - 1)
-        multiply(0, j)
+        for tile in early:
+            if j > 1:
+                products.reduce(tile, j - 1)
+        for tile in early:
+            multiply(tile, j)
         if j == 0:
-            products.reduce(0, 0)
-    products.pass_on(0)
-    columns.pass_across(range(6, NZ))
-    for tile in range(1, NY):
+            for tile in early:
+                products.reduce(tile, 0)
+    for tile in early:
+        products.pass_on(tile)
+    for tile in early:
+        products.reduce(tile, 3)
+    for tile in (2, 3):
         columns.await_tile(tile)
         for j in range(RING_X):
             multiply(tile, j)
-        products.reduce(tile - 1, 3)
         products.reduce(tile, 0)
-        if tile > 1:
+        if tile > 2:
             products.pass_on(tile - 1)
         products.reduce(tile, 1)
         products.reduce(tile, 2)
+        products.reduce(tile, 3)
     products.pass_on(NY - 1)
-    products.reduce(NY - 1, 3)
     for tile in range(NY):
         products.last(tile, out)
     copies.finish()
@@ -694,7 +698,7 @@
     turns = rotation_tables(near)
     return pl.pallas_call(
         block_kernel,
-        out_shape=jax.ShapeDtypeStruct((count, width), bf16),
+        out_shape=pltpu.VMEM((count, width), bf16),
         in_specs=[pl.BlockSpec(memory_space=pltpu.SMEM)] + [vmem] * 10,
         out_specs=vmem,
         scratch_shapes=[
@@ -721,7 +725,7 @@
             pltpu.SemaphoreType.DMA((COPIES,)),
         ],
         compiler_params=pltpu.CompilerParams(
-            collective_id=0, has_side_effects=True, vmem_limit_bytes=60 * 1024 * 1024
+            collective_id=0, has_side_effects=True, vmem_limit_bytes=54 * 1024 * 1024
         ),
     )(doc_blocks, tokens, gain, w_query, w_key, w_value, w_out_t, *turns)
 

time: 136 us -> 133 us (0.978)
  Pallas kernels: 132 us -> 130 us
    pallas_call x1, Pallas kernels: 132 us -> 130 us  [whole_block(): pl.pallas_call(block_kernel, out_shape=pltpu.VMEM((count, width), bf16),...]
where the time goes in v5:
time: 133 us; the launch traced here: 131 us
  Pallas kernels  130 us (98%)
    pallas_call x1, Pallas kernels, whole_block(): pl.pallas_call(block_kernel, out_shape=pltpu.VMEM((count, width), bf16),...  130 us

profile of v5, /device:TPU:38, one launch (start us, length us, event | category | flops | bytes accessed | tf_op | source)
XLA Modules:
  0.0 130.9 jit_solution(400187928227895259)
XLA Ops:
  0.0 129.9 %shard_map.109 = bf16[128,4096]{1,0:T(8,128)(2,1)S(1)} custom-call(s32[256]{0:T(256)} %docs.1, bf16[128,4096]{1,0:T(8,128)(2,1)} %tokens.1, f32[1,4096]{1,0:T(1,128)} %bitcast.3, bf16[64,1024]{1,0:T(8,128)(2,1)} %wq.1, bf16[64,128]{1,0:T(8,128)(2,1)} %wk.1, bf16[64,128]{1,0:T(8,128)(2,1)} %wv.1, bf16[64,1024]{1,0:T(8,128)(2,1)} %bitcast.2, ...), custom_call_target="tpu_custom_call" | custom-call | tf_op jit(solution)/shard_map/pallas_call | solution.py:699
  129.9 1.0 copy.13

commit v6 on v5

--- a/solution.py
+++ b/solution.py
@@ -529,8 +529,6 @@
 
     for stage in range(max(len(plan) for plan in plans)):
         run(stage)
-        if stage == 0:
-            fill_tables()
         if stage == 1:
             columns.ring_begin()
         if stage == 2:
@@ -542,6 +540,7 @@
     gathers[0].rest()
     gathers[1].rest()
     columns.send_across(-1, range(7))
+    fill_tables()
     token_rows.second_hop()
     token_rows.rest()
 

time: 133 us -> 133 us (level)
  no operation moved by 1% of the time
where the time goes in v6:
time: 133 us; the launch traced here: 131 us
  Pallas kernels  130 us (98%)
    pallas_call x1, Pallas kernels, whole_block(): pl.pallas_call(block_kernel, out_shape=pltpu.VMEM((count, width), bf16),...  130 us

profile of v6, /device:TPU:38, one launch (start us, length us, event | category | flops | bytes accessed | tf_op | source)
XLA Modules:
  0.0 130.9 jit_solution(3080246690209833102)
XLA Ops:
  0.0 129.9 %shard_map.109 = bf16[128,4096]{1,0:T(8,128)(2,1)S(1)} custom-call(s32[256]{0:T(256)} %docs.1, bf16[128,4096]{1,0:T(8,128)(2,1)} %tokens.1, f32[1,4096]{1,0:T(1,128)} %bitcast.3, bf16[64,1024]{1,0:T(8,128)(2,1)} %wq.1, bf16[64,128]{1,0:T(8,128)(2,1)} %wk.1, bf16[64,128]{1,0:T(8,128)(2,1)} %wv.1, bf16[64,1024]{1,0:T(8,128)(2,1)} %bitcast.2, ...), custom_call_target="tpu_custom_call" | custom-call | tf_op jit(solution)/shard_map/pallas_call | solution.py:698
  129.9 1.0 copy.13
